TPU v7x, 512 devices: a whole 4x8x8 slice. The times are simulated.
512 devices in a mesh: pipe: 16 (over x_hi, z), tensor: 8 (over y), dp: 4 (over x_lo, core).
Axes of the slice: x: 4 (x_hi: 2, x_lo: 2; x = x_hi * 2 + x_lo), y: 8, z: 8, core: 2. Of those that a mesh axis runs over, the one named last changes fastest.
Arguments:
- sent_act: bfloat16 [4, 16, 256, 12288], P('dp', 'pipe', None, 'tensor'), may hold values from -64 to 64
- sent_grad: bfloat16 [4, 16, 256, 12288], P('dp', 'pipe', None, 'tensor'), may hold values from -64 to 64
- evicted: bfloat16 [4, 16, 256, 12288], P('dp', 'pipe', None, 'tensor'), may hold values from -64 to 64
- layer_params: float32 [16, 3, 12288], P('pipe', None, 'tensor'), may hold values from -8 to 8
- doc_ids: int32 [4, 16, 2, 256], P('dp', 'pipe'), may hold values from 0 to 3, never falling along the last dimension, each value on 1 to 128 neighbouring positions
Outputs:
- new_act: bfloat16 [4, 16, 256, 12288], P('dp', 'pipe', None, 'tensor')
- new_grad: bfloat16 [4, 16, 256, 12288], P('dp', 'pipe', None, 'tensor')
- kept_input: bfloat16 [4, 16, 256, 12288], P('dp', 'pipe', None, 'tensor')
- param_grad: float32 [16, 3, 12288], P('pipe', None, 'tensor')
All inputs are finite; a program needn't handle non-finite values.
Results may differ from a plain program's by a relative error of at most 0.0025.
The roundings to bfloat16 on the way count: a program that leaves them out, or rounds other values in their place, can miss the bound.
Values may be sent and summed in bfloat16 or wider, within the bound.
No kernel may reach another device: no remote copies, remote signals or barrier semaphores. Data moves between devices by JAX's collectives and lax.ppermute only.
A program may use at most 64 MiB of HBM per device.

v0:
```python
import jax
import jax.numpy as jnp
from jax import lax
from jax.sharding import PartitionSpec as P

D = 12288
HEAD = 128


EPS = 1e-05


def from_behind(block, axis, distance):
    devices = range(lax.axis_size(axis))
    route = [((i - distance) % len(devices), i) for i in devices]
    return lax.ppermute(block, axis, route)


def normalize(block):
    values = block.astype(jnp.float32)
    row_sum = lax.psum(jnp.sum(values, 1), "tensor")
    centred = values - (row_sum / D)[:, None]
    spread = lax.psum(jnp.sum(centred * centred, 1), "tensor") / D
    scaling = lax.rsqrt(spread + EPS)[:, None]
    return (centred * scaling, scaling, values)


def project(unit, params):
    hidden = unit * params[0]
    count = unit.shape[0]
    query = (hidden * params[1]).astype(jnp.bfloat16).reshape(count, -1, HEAD)
    keyed = (hidden * params[2]).astype(jnp.bfloat16).reshape(count, -1, HEAD)
    valued = hidden.astype(jnp.bfloat16).reshape(count, -1, HEAD)
    return (hidden, query, keyed, valued)


def probabilities(query, keyed, docs):
    scores = jnp.einsum(
        "thd,shd->hts", query, keyed, preferred_element_type=jnp.float32
    ) * HEAD ** (-0.5)
    position = jnp.arange(docs.shape[0])
    allowed = (position[None, :] <= position[:, None]) & (docs[None, :] == docs[:, None])
    scores = jnp.where(allowed[None], scores, -1e30)
    peak = jnp.max(scores, -1, keepdims=True)
    weights = jnp.exp(scores - peak)
    return weights / jnp.sum(weights, -1, keepdims=True)


def forward_layer(block, docs, params):
    unit, scaling, values = normalize(block)
    hidden, query, keyed, valued = project(unit, params)
    probs = probabilities(query, keyed, docs)
    mixed = jnp.einsum(
        "hts,shd->thd", probs.astype(jnp.bfloat16), valued, preferred_element_type=jnp.float32
    )
    return (values + mixed.reshape(block.shape[0], -1)).astype(jnp.bfloat16)


def backward_layer(block, upstream, docs, params):
    count = block.shape[0]
    unit, scaling, values = normalize(block)
    hidden, query, keyed, valued = project(unit, params)
    probs = probabilities(query, keyed, docs)
    upper = upstream.reshape(count, -1, HEAD)
    grad_vals = jnp.einsum(
        "hts,thd->shd", probs.astype(jnp.bfloat16), upper, preferred_element_type=jnp.float32
    )
    grad_probs = jnp.einsum("thd,shd->hts", upper, valued, preferred_element_type=jnp.float32)
    centre = jnp.sum(grad_probs * probs, -1, keepdims=True)
    grad_scores = (probs * (grad_probs - centre)).astype(jnp.bfloat16)
    grad_query = jnp.einsum(
        "hts,shd->thd", grad_scores, keyed, preferred_element_type=jnp.float32
    ) * HEAD ** (-0.5)
    grad_keys = jnp.einsum(
        "hts,thd->shd", grad_scores, query, preferred_element_type=jnp.float32
    ) * HEAD ** (-0.5)
    grad_query = grad_query.reshape(count, -1)
    grad_keys = grad_keys.reshape(count, -1)
    grad_hidden = grad_query * params[1] + grad_keys * params[2] + grad_vals.reshape(count, -1)
    grad_unit = grad_hidden * params[0]
    sum_grad, sum_cross = lax.psum((jnp.sum(grad_unit, 1), jnp.sum(grad_unit * unit, 1)), "tensor")
    result = scaling * (
        grad_unit - (sum_grad / D)[:, None] - unit * (sum_cross / D)[:, None]
    ) + upstream.astype(jnp.float32)
    section_grad = jnp.stack(
        [
            jnp.sum(grad_hidden * unit, 0),
            jnp.sum(grad_query * hidden, 0),
            jnp.sum(grad_keys * hidden, 0),
        ]
    )
    return (result.astype(jnp.bfloat16), section_grad)


def spread_mirror(leading, trailing):
    part_count = lax.axis_size("pipe")
    row_count = leading.shape[0]
    width = leading.shape[1]
    lead_parts = leading.reshape(part_count, row_count // part_count, width)
    trail_parts = trailing.reshape(part_count, row_count // part_count, width)
    lead_parts, trail_parts = (
        lax.all_to_all(lead_parts, "pipe", split_axis=0, concat_axis=0, tiled=True),
        lax.all_to_all(trail_parts, "pipe", split_axis=0, concat_axis=0, tiled=True),
    )
    lead_parts = jnp.flip(lead_parts, 0)
    trail_parts = jnp.flip(trail_parts, 0)
    lead_parts, trail_parts = (
        lax.all_to_all(lead_parts, "pipe", split_axis=0, concat_axis=0, tiled=True),
        lax.all_to_all(trail_parts, "pipe", split_axis=0, concat_axis=0, tiled=True),
    )
    return (lead_parts.reshape(row_count, width), trail_parts.reshape(row_count, width))


def local(sent_act, sent_grad, evicted, layer_params, doc_ids):
    fwd_in = from_behind(sent_act[0, 0], "pipe", 1)
    up_grad = from_behind(sent_grad[0, 0], "pipe", -1)
    held_stash = evicted[0, 0]
    kept_input, bwd_in = spread_mirror(fwd_in, held_stash)
    params = layer_params[0]
    new_act = forward_layer(fwd_in, doc_ids[0, 0, 0], params)
    new_grad, section_grad = backward_layer(bwd_in, up_grad, doc_ids[0, 0, 1], params)
    summed = lax.psum(section_grad, "dp")
    return (new_act[None, None], new_grad[None, None], kept_input[None, None], summed[None])


def solution(mesh):
    in_specs = (
        P("dp", "pipe", None, "tensor"),
        P("dp", "pipe", None, "tensor"),
        P("dp", "pipe", None, "tensor"),
        P("pipe", None, "tensor"),
        P("dp", "pipe", None, None),
    )
    out_specs = (
        P("dp", "pipe", None, "tensor"),
        P("dp", "pipe", None, "tensor"),
        P("dp", "pipe", None, "tensor"),
        P("pipe", None, "tensor"),
    )
    return jax.shard_map(local, mesh=mesh, in_specs=in_specs, out_specs=out_specs, check_vma=False)
```

profile of v0, /device:TPU:1, one launch (start us, length us, event | category | flops | bytes accessed | tf_op | source)
XLA Modules:
  0.0 217.3 jit_solution(2130587558893051965)
XLA Ops:
  0.6 0.0 copy-start.6
  0.6 13.6 %all-to-all-start = ((bf16[16,16,1536]{2,1,0:T(8,128)(2,1)}), bf16[16,16,1536]{2,1,0:T(8,128)(2,1)S(1)}, u32[]{:S(2)}, u32[]{:S(2)}) async-start(bf16[16,16,1536]{2,1,0:T(8,128)(2,1)} %bitcast.107), calls=%async_computation | async-start | bytes 1572864 | tf_op jit(solution)/shard_map/all_to_all | solution.py:103
  14.2 0.0 copy-done.6
  14.2 0.3 copy.43
  14.5 3.3 %collective-permute-start = (bf16[256,1536]{0,1:T(8,128)(2,1)S(1)}, bf16[256,1536]{0,1:T(8,128)(2,1)S(1)}, u32[]{:S(2)}, u32[]{:S(2)}) collective-permute-start(bf16[256,1536]{0,1:T(8,128)(2,1)S(1)} %bitcast.109), channel_id=1, source_target_pairs={{480,0},{0,32},{32,64},{64,96},{96,128},{128,160},{160,192},{192,2... | collective-permute-start | bytes 2359304 | tf_op jit(solution)/shard_map/ppermute | solution.py:16
  17.8 35.5 %collective-permute-done = bf16[256,1536]{0,1:T(8,128)(2,1)S(1)} collective-permute-done((bf16[256,1536]{0,1:T(8,128)(2,1)S(1)}, bf16[256,1536]{0,1:T(8,128)(2,1)S(1)}, u32[]{:S(2)}, u32[]{:S(2)}) %collective-permute-start) | collective-permute-done | bytes 786464 | tf_op jit(solution)/shard_map/ppermute | solution.py:16
  53.3 1.2 copy.57
  54.5 0.0 all-to-all-done
  54.5 5.3 %all-to-all-start.2 = ((bf16[16,16,1536]{2,1,0:T(8,128)(2,1)}), bf16[16,16,1536]{2,1,0:T(8,128)(2,1)S(1)}, u32[]{:S(2)}, u32[]{:S(2)}) async-start(bf16[16,16,1536]{2,1,0:T(8,128)(2,1)} %bitcast.22), calls=%async_computation.2 | async-start | bytes 1572864 | tf_op jit(solution)/shard_map/all_to_all | solution.py:102
  59.8 0.0 copy-start.7
  59.8 0.9 rev.7
  60.7 20.0 %all-to-all-done.2 = bf16[16,16,1536]{2,1,0:T(8,128)(2,1)S(1)} async-done(((bf16[16,16,1536]{2,1,0:T(8,128)(2,1)}), bf16[16,16,1536]{2,1,0:T(8,128)(2,1)S(1)}, u32[]{:S(2)}, u32[]{:S(2)}) %all-to-all-start.2) | async-done | bytes 786464 | tf_op jit(solution)/shard_map/all_to_all | solution.py:102
  80.7 6.5 %all-to-all-start.1 = ((bf16[16,16,1536]{2,1,0:T(8,128)(2,1)}), bf16[16,16,1536]{2,1,0:T(8,128)(2,1)S(1)}, u32[]{:S(2)}, u32[]{:S(2)}) async-start(bf16[16,16,1536]{2,1,0:T(8,128)(2,1)} %rev.7), calls=%async_computation.1 | async-start | bytes 1572864 | tf_op jit(solution)/shard_map/all_to_all | solution.py:109
  87.3 0.0 copy-done.7
  87.3 1.2 copy.50
  88.4 6.9 %collective-permute-start.1 = (bf16[256,1536]{0,1:T(8,128)(2,1)}, bf16[256,1536]{0,1:T(8,128)(2,1)}, u32[]{:S(2)}, u32[]{:S(2)}) collective-permute-start(bf16[256,1536]{0,1:T(8,128)(2,1)} %bitcast.108), channel_id=1, source_target_pairs={{32,0},{64,32},{96,64},{128,96},{160,128},{192,160},{224,192},{256... | collective-permute-start | bytes 2359304 | tf_op jit(solution)/shard_map/ppermute | solution.py:16
  95.3 0.0 copy-done.8
  95.3 0.1 slice_reduce_fusion
  95.4 0.0 copy-done.9
  95.4 0.1 fusion.39
  95.5 0.1 fusion.40
  95.6 0.2 convert_reduce_fusion
  95.9 0.9 rev.8
  96.8 11.4 %all-to-all-done.1 = bf16[16,16,1536]{2,1,0:T(8,128)(2,1)S(1)} async-done(((bf16[16,16,1536]{2,1,0:T(8,128)(2,1)}), bf16[16,16,1536]{2,1,0:T(8,128)(2,1)S(1)}, u32[]{:S(2)}, u32[]{:S(2)}) %all-to-all-start.1) | async-done | bytes 786464 | tf_op jit(solution)/shard_map/all_to_all | solution.py:109
  108.2 6.5 %all-to-all-start.3 = ((bf16[16,16,1536]{2,1,0:T(8,128)(2,1)}), bf16[16,16,1536]{2,1,0:T(8,128)(2,1)}, u32[]{:S(2)}, u32[]{:S(2)}) async-start(bf16[16,16,1536]{2,1,0:T(8,128)(2,1)} %rev.8), calls=%async_computation.3 | async-start | bytes 1572864 | tf_op jit(solution)/shard_map/all_to_all | solution.py:108
  114.7 0.2 convert_reduce_fusion.1
  114.9 0.1 reduce_sum.116
  115.0 14.7 %psum.51 = f32[256]{0:T(256)S(1)} all-reduce(f32[256]{0:T(256)S(1)} %reduce_sum.116), channel_id=1, replica_groups=mesh['pipe'=16,'tensor'=8,'dp'=4] {'tensor'}, use_global_device_ids=true, to_apply=%region_7.8 | all-reduce | flops 256 | bytes 2048 | tf_op jit(solution)/shard_map/psum | solution.py:21
  129.7 0.1 sub.73
  129.8 0.3 multiply_reduce_fusion.2
  130.1 0.1 reduce_sum.118
  130.2 1.8 reshape.309
  132.1 1.8 copy.47
  133.9 0.0 copy-start
  133.9 12.1 %all-reduce.1 = (f32[256]{0:T(256)S(1)}, f32[256]{0:T(256)S(1)}) all-reduce(f32[256]{0:T(256)S(1)} %convert_reduce_fusion, f32[256]{0:T(256)S(1)} %reduce_sum.118), channel_id=1, replica_groups=mesh['pipe'=16,'tensor'=8,'dp'=4] {'tensor'}, use_global_device_ids=true, to_apply=%region_1.2 | all-reduce | flops 512 | bytes 4096 | tf_op jit(solution)/shard_map/psum | solution.py:21
  146.0 1.7 multiply_convert_fusion.1
  147.7 4.2 %fusion.50 = (f32[12,256]{1,0:T(8,128)S(1)}, f32[12,256,256]{1,2,0:T(8,128)}) fusion(pred[256,256]{0,1:T(8,128)(4,1)S(1)} %fusion.39, bf16[256,12,128]{0,2,1:T(8,128)(2,1)} %get-tuple-element.26, bf16[256,12,128]{0,2,1:T(8,128)(2,1)} %get-tuple-element.25), kind=kOutput, calls=%fused_computation.90 | convolution fusion | flops 204472576 | bytes 4796416 | tf_op jit(solution)/shard_map/sub | solution.py:45
  151.9 0.0 collective-permute-done.1
  151.9 0.0 copy-done
  151.9 3.2 %fusion.2 = (f32[12,256]{1,0:T(8,128)S(1)}, f32[12,256,256]{2,1,0:T(8,128)S(1)}) fusion(f32[12,256,256]{1,2,0:T(8,128)} %get-tuple-element.34, f32[12,256]{1,0:T(8,128)S(1)} %get-tuple-element.33, bf16[256,12,128]{0,2,1:T(8,128)(2,1)} %bitcast.11, f32[12,128]{1,0:T(8,128)S(1)} %bitcast.113, f32[256]{0:T(256)S(1)} %get-tuple-element.48, ...), kind=kOutput, calls=%fused_computation.4 | convolution fusion | flops 205255680 | bytes 8683520 | tf_op jit(solution)/shard_map/thd,shd->hts/dot_general | solution.py:68
  155.1 0.0 copy-done.2
  155.1 0.0 copy-start.4
  155.1 0.6 fusion.4
  155.7 0.5 copy-done.4
  156.2 0.6 broadcast_multiply_fusion
  156.9 0.5 copy-done.3
  157.4 1.6 broadcast_multiply_fusion.1
  158.9 0.0 copy-done.1
  158.9 4.1 %multiply_reduce_fusion = (f32[12,128]{1,0:T(8,128)S(1)}, f32[256]{0:T(256)S(1)}, f32[12,128]{1,0:T(8,128)S(1)}, f32[12,128]{1,0:T(8,128)S(1)}, f32[256]{0:T(256)S(1)}, /*index=5*/f32[12,256,128]{1,2,0:T(8,128)}) fusion(f32[256,12,128]{0,2,1:T(8,128)S(1)} %copy-done.1, f32[256]{0:T(256)S(1)} %get-tuple-element.48, f32[256]{0:T(256)S(1)} %broadcast_multiply_fusion.6, ...), kind=kOutput, calls=%fused_computation.42 | convolution fusion | flops 210365440 | bytes 10276864 | tf_op jit(solution)/shard_map/hts,thd->shd/dot_general | solution.py:65
  163.1 0.3 fusion.9
  163.3 11.8 %all-reduce = (f32[256]{0:T(256)S(1)}, f32[256]{0:T(256)S(1)}, f32[256]{0:T(256)S(1)}) all-reduce(f32[256]{0:T(256)S(1)} %fusion.9, f32[256]{0:T(256)S(1)} %get-tuple-element.13, f32[256]{0:T(256)S(1)} %get-tuple-element.16), channel_id=1, replica_groups=mesh['pipe'=16,'tensor'=8,'dp'=4] {'tensor'}, use_global_device_ids=true, to_apply=%region_3.4 | all-reduce | flops 768 | bytes 6144 | tf_op jit(solution)/shard_map/psum | solution.py:23
  175.1 1.4 convert_element_type.70
  176.5 3.0 %copy.56 = f32[256,1536]{0,1:T(8,128)} copy(f32[256,1536]{1,0:T(8,128)} %bitcast.101) | data formatting | bytes 3145728 | tf_op jit(solution)/shard_map/convert_element_type | solution.py:20
  179.5 5.1 %fusion.15 = (bf16[256,1536]{0,1:T(8,128)(2,1)}, bf16[256,1536]{0,1:T(8,128)(2,1)}, bf16[256,1536]{0,1:T(8,128)(2,1)}, bf16[256,1536]{0,1:T(8,128)(2,1)S(1)}) fusion(bf16[256,1536]{0,1:T(8,128)(2,1)S(1)} %collective-permute-done, f32[1536]{0:T(1024)S(1)} %get-tuple-element.17, f32[1536]{0:T(1024)S(1)} %get-tuple-element.18, f32[256]{0:T(256)S(1)} %add_rsqrt_fusion.1, ...), kind=kLoop, calls=%fused_computation.25 | loop fusion | flops 9043968 | bytes 11034624 | tf_op jit(solution)/shard_map/convert_element_type | solution.py:32
  184.7 0.0 copy-start.5
  184.7 4.3 %fusion.51 = (f32[12,256]{1,0:T(8,128)S(1)}, f32[12,256,256]{1,2,0:T(8,128)}) fusion(pred[256,256]{0,1:T(8,128)(4,1)S(1)} %fusion.40, bf16[256,12,128]{0,2,1:T(8,128)(2,1)} %bitcast.106, bf16[256,12,128]{0,2,1:T(8,128)(2,1)} %bitcast.105), kind=kOutput, calls=%fused_computation.91 | convolution fusion | flops 204472576 | bytes 4796416 | tf_op jit(solution)/shard_map/sub | solution.py:45
  189.0 0.0 copy-done.5
  189.0 2.3 %fusion.32 = f32[12,128,256]{2,1,0:T(8,128)S(1)} fusion(bf16[256,12,128]{0,2,1:T(8,128)(2,1)S(1)} %bitcast.104, f32[12,256,256]{1,2,0:T(8,128)} %get-tuple-element.45, f32[12,256]{1,0:T(8,128)S(1)} %get-tuple-element.44), kind=kOutput, calls=%fused_computation.55 | convolution fusion | flops 202899456 | bytes 5517312 | tf_op jit(solution)/shard_map/hts,shd->thd/dot_general | solution.py:53
  191.3 0.2 fusion.16
  191.5 1.2 copy.58
  192.7 1.2 copy.59
  193.8 21.4 %psum.55 = f32[1,3,1536]{2,0,1:T(1,128)} all-reduce(f32[1,3,1536]{2,0,1:T(1,128)S(1)} %broadcast_in_dim.49), channel_id=1, replica_groups=mesh['pipe'=16,'tensor'=8,'dp'=4] {'dp'}, use_global_device_ids=true, to_apply=%region_20.21 | all-reduce | flops 4608 | bytes 36864 | tf_op jit(solution)/shard_map/psum | solution.py:122
  215.2 0.0 all-to-all-done.3
  215.2 2.1 copy.80
  (17 shorter events, 0.1 us)
Async XLA Ops:
  0.6 13.6 %copy-start.6 = (bf16[1,1,256,1536]{3,2,1,0:T(8,128)(2,1)S(1)}, bf16[1,1,256,1536]{3,2,1,0:T(8,128)(2,1)}, u32[]{:S(2)}) copy-start(bf16[1,1,256,1536]{3,2,1,0:T(8,128)(2,1)} %param.5) | copy-start | bytes 2359300
  0.6 53.8 %all-to-all-start = ((bf16[16,16,1536]{2,1,0:T(8,128)(2,1)}), bf16[16,16,1536]{2,1,0:T(8,128)(2,1)S(1)}, u32[]{:S(2)}, u32[]{:S(2)}) async-start(bf16[16,16,1536]{2,1,0:T(8,128)(2,1)} %bitcast.107), calls=%async_computation | async-start | bytes 1572864 | tf_op jit(solution)/shard_map/all_to_all | solution.py:103
  14.5 38.8 %collective-permute-start = (bf16[256,1536]{0,1:T(8,128)(2,1)S(1)}, bf16[256,1536]{0,1:T(8,128)(2,1)S(1)}, u32[]{:S(2)}, u32[]{:S(2)}) collective-permute-start(bf16[256,1536]{0,1:T(8,128)(2,1)S(1)} %bitcast.109), channel_id=1, source_target_pairs={{480,0},{0,32},{32,64},{64,96},{96,128},{128,160},{160,192},{192,2... | collective-permute-start | bytes 2359304 | tf_op jit(solution)/shard_map/ppermute | solution.py:16
  54.5 26.3 %all-to-all-start.2 = ((bf16[16,16,1536]{2,1,0:T(8,128)(2,1)}), bf16[16,16,1536]{2,1,0:T(8,128)(2,1)S(1)}, u32[]{:S(2)}, u32[]{:S(2)}) async-start(bf16[16,16,1536]{2,1,0:T(8,128)(2,1)} %bitcast.22), calls=%async_computation.2 | async-start | bytes 1572864 | tf_op jit(solution)/shard_map/all_to_all | solution.py:102
  59.8 27.5 %copy-start.7 = (bf16[1,1,256,1536]{3,2,1,0:T(8,128)(2,1)S(1)}, bf16[1,1,256,1536]{3,2,1,0:T(8,128)(2,1)}, u32[]{:S(2)}) copy-start(bf16[1,1,256,1536]{3,2,1,0:T(8,128)(2,1)} %param.6) | copy-start | bytes 2359300
  60.7 34.6 %copy-start.8 = (f32[1,3,1536]{2,0,1:T(1,128)S(1)}, f32[1,3,1536]{2,0,1:T(1,128)}, u32[]{:S(2)}) copy-start(f32[1,3,1536]{2,0,1:T(1,128)} %param.8) | copy-start | bytes 55300
  60.7 34.7 %copy-start.9 = (s32[1,1,2,256]{3,2,1,0:T(2,128)S(1)}, s32[1,1,2,256]{3,2,1,0:T(2,128)}, u32[]{:S(2)}) copy-start(s32[1,1,2,256]{3,2,1,0:T(2,128)} %param.9) | copy-start | bytes 6148
  80.7 27.5 %all-to-all-start.1 = ((bf16[16,16,1536]{2,1,0:T(8,128)(2,1)}), bf16[16,16,1536]{2,1,0:T(8,128)(2,1)S(1)}, u32[]{:S(2)}, u32[]{:S(2)}) async-start(bf16[16,16,1536]{2,1,0:T(8,128)(2,1)} %rev.7), calls=%async_computation.1 | async-start | bytes 1572864 | tf_op jit(solution)/shard_map/all_to_all | solution.py:109
  88.4 63.5 %collective-permute-start.1 = (bf16[256,1536]{0,1:T(8,128)(2,1)}, bf16[256,1536]{0,1:T(8,128)(2,1)}, u32[]{:S(2)}, u32[]{:S(2)}) collective-permute-start(bf16[256,1536]{0,1:T(8,128)(2,1)} %bitcast.108), channel_id=1, source_target_pairs={{32,0},{64,32},{96,64},{128,96},{160,128},{192,160},{224,192},{256... | collective-permute-start | bytes 2359304 | tf_op jit(solution)/shard_map/ppermute | solution.py:16
  108.2 107.0 %all-to-all-start.3 = ((bf16[16,16,1536]{2,1,0:T(8,128)(2,1)}), bf16[16,16,1536]{2,1,0:T(8,128)(2,1)}, u32[]{:S(2)}, u32[]{:S(2)}) async-start(bf16[16,16,1536]{2,1,0:T(8,128)(2,1)} %rev.8), calls=%async_computation.3 | async-start | bytes 1572864 | tf_op jit(solution)/shard_map/all_to_all | solution.py:108
  133.9 18.0 %copy-start = (f32[256,12,128]{0,2,1:T(8,128)}, f32[256,12,128]{0,2,1:T(8,128)S(1)}, u32[]{:S(2)}) copy-start(f32[256,12,128]{0,2,1:T(8,128)S(1)} %copy.47) | copy-start | bytes 4718596
  151.9 3.2 %copy-start.2 = (f32[12,256,256]{1,2,0:T(8,128)S(1)}, f32[12,256,256]{1,2,0:T(8,128)}, u32[]{:S(2)}) copy-start(f32[12,256,256]{1,2,0:T(8,128)} %get-tuple-element.34) | copy-start | bytes 9437188
  155.1 1.1 copy-start.4
  156.2 1.1 copy-start.3
  157.4 1.6 copy-start.1
  184.7 4.3 %copy-start.5 = (bf16[256,1536]{0,1:T(8,128)(2,1)S(1)}, bf16[256,1536]{0,1:T(8,128)(2,1)}, u32[]{:S(2)}) copy-start(bf16[256,1536]{0,1:T(8,128)(2,1)} %get-tuple-element.29) | copy-start | bytes 2359300
where the time goes:
time: 218 us; the launch traced here: 217 us
  waiting for transfers between devices  66.9 us (31%)
  blocking collectives  60 us (28%)
  starting transfers between devices  42.1 us (19%)
  matrix products  20.2 us (9%)
  local copies, waits for them, and re-layouts  16.9 us (8%)
  other arithmetic  10.2 us (5%)
    ppermute x2, waiting for transfers between devices, from_behind(): return lax.ppermute(block, axis, route)  35.5 us
    psum x2, blocking collectives, normalize(): row_sum = lax.psum(jnp.sum(values, 1), 'tensor')  26.8 us
    psum x1, blocking collectives, local(): summed = lax.psum(section_grad, 'dp')  21.4 us
    all_to_all x2, starting transfers between devices, spread_mirror(): lax.all_to_all(trail_parts, 'pipe', split_axis=0, concat_axis=0, tiled=True)  20.1 us
    all_to_all x2, waiting for transfers between devices, spread_mirror(): lax.all_to_all(lead_parts, 'pipe', split_axis=0, concat_axis=0, tiled=True)  20 us
    all_to_all x2, starting transfers between devices, spread_mirror(): lax.all_to_all(lead_parts, 'pipe', split_axis=0, concat_axis=0, tiled=True)  11.8 us
    psum x1, blocking collectives, normalize(): spread = lax.psum(jnp.sum(centred * centred, 1), 'tensor') / D  11.8 us
    all_to_all x2, waiting for transfers between devices, spread_mirror(): lax.all_to_all(trail_parts, 'pipe', split_axis=0, concat_axis=0, tiled=True)  11.4 us
  transfers between devices with their start and end apart: 6, of which 3 were waited for; matrix products, arithmetic and copies ran while one was open for 20% of the time, Pallas kernels for 0%

commit v1 on v0

v1 whole, which is shorter than its diff:
```python
import jax
import jax.numpy as jnp
from jax import lax
from jax.experimental import pallas as pl
from jax.experimental.pallas import tpu as pltpu
from jax.sharding import PartitionSpec as P

D = 12288
HEAD = 128
TOK = 256
N_TENSOR = 8
WIDTH = D // N_TENSOR
HEADS = WIDTH // HEAD
SCALE = HEAD ** (-0.5)
EPS = 1e-05
ACT, STASH = 0, 16
F32 = jnp.float32
BF16 = jnp.bfloat16


def move(block, route):
    count = lax.axis_size("pipe")
    return lax.ppermute(block, "pipe", [(j, route(j) % count) for j in range(count)])


def dot(left, right, dims):
    return lax.dot_general(left, right, (dims, ((), ())), preferred_element_type=F32)


def as_rows(first, second):
    lane = lax.broadcasted_iota(jnp.int32, (TOK, HEAD), 1)
    return jnp.transpose(jnp.where(lane == 0, first, second))[0:8]


def as_columns(first, second):
    row = lax.broadcasted_iota(jnp.int32, (HEAD, TOK), 0)
    both = jnp.transpose(jnp.where(row == 0, first, second))
    return both[:, 0:1], both[:, 1:2]


def stats_kernel(place_ref, act_ref, stash_ref, out_ref):
    place = place_ref[0]
    row = lax.broadcasted_iota(jnp.int32, (N_TENSOR, TOK), 0)
    for ref, start in ((act_ref, ACT), (stash_ref, STASH)):
        total = jnp.zeros((TOK, HEAD), F32)
        for h in range(HEADS):
            total = total + ref[:, h * HEAD:(h + 1) * HEAD].astype(F32)
        total = jnp.sum(total, 1, keepdims=True)
        mean = total / WIDTH
        spread = jnp.zeros((TOK, HEAD), F32)
        for h in range(HEADS):
            centred = ref[:, h * HEAD:(h + 1) * HEAD].astype(F32) - mean
            spread = spread + centred * centred
        rows = as_rows(total, jnp.sum(spread, 1, keepdims=True))
        out_ref[start:start + 8] = jnp.where(row == place, rows[0:1], 0.0)
        out_ref[start + 8:start + 16] = jnp.where(row == place, rows[1:2], 0.0)


def local_stats(place, act, stash):
    return pl.pallas_call(
        stats_kernel,
        in_specs=[pl.BlockSpec(memory_space=pltpu.SMEM)] + [pl.BlockSpec(memory_space=pltpu.VMEM)] * 2,
        out_specs=pl.BlockSpec(memory_space=pltpu.VMEM),
        out_shape=jax.ShapeDtypeStruct((4 * N_TENSOR, TOK), F32),
        cost_estimate=pl.CostEstimate(flops=8 * TOK * WIDTH, bytes_accessed=4 * TOK * WIDTH, transcendentals=0),
        compiler_params=pltpu.CompilerParams(vmem_limit_bytes=16 * 2**20),
        name="local_stats",
    )(place, act, stash)


def mean_and_scaling(stats_ref, start):
    sums, squares = stats_ref[start:start + 8], stats_ref[start + 8:start + 16]
    mean = jnp.sum(sums, 0, keepdims=True) / D
    apart = sums / WIDTH - mean
    spread = (jnp.sum(squares, 0, keepdims=True) + WIDTH * jnp.sum(apart * apart, 0, keepdims=True)) / D
    return as_columns(mean, lax.rsqrt(spread + EPS))


def prepare(start, stats_ref, docs_ref, mean_ref, scaling_ref, bias_ref):
    mean, scaling = mean_and_scaling(stats_ref, start)
    mean_ref[...] = jnp.broadcast_to(mean, (TOK, HEAD))
    scaling_ref[...] = jnp.broadcast_to(scaling, (TOK, HEAD))
    docs = docs_ref[...].astype(F32)
    column, _ = as_columns(docs, docs)
    t = lax.broadcasted_iota(jnp.int32, (TOK, TOK), 0)
    u = lax.broadcasted_iota(jnp.int32, (TOK, TOK), 1)
    bias_ref[...] = jnp.where((u <= t) & (column == docs), 0.0, -1e30)


def project(values, mean_ref, scaling_ref, params):
    unit = (values - mean_ref[...]) * scaling_ref[...]
    hidden = unit * params[0:1]
    query = (hidden * params[1:2]).astype(BF16)
    keyed = (hidden * params[2:3]).astype(BF16)
    return unit, hidden, query, keyed, hidden.astype(BF16)


def probabilities(query, keyed, bias_ref):
    scores = dot(query, keyed, ((1,), (1,))) * SCALE + bias_ref[...]
    weights = jnp.exp(scores - jnp.max(scores, 1, keepdims=True))
    return weights * (1.0 / jnp.sum(weights, 1, keepdims=True))


def forward_kernel(stats_ref, docs_ref, params_ref, x_ref, out_ref, mean_ref, scaling_ref, bias_ref):
    @pl.when(pl.program_id(0) == 0)
    def _():
        prepare(ACT, stats_ref, docs_ref, mean_ref, scaling_ref, bias_ref)

    for i in range(x_ref.shape[1] // HEAD):
        part = slice(i * HEAD, (i + 1) * HEAD)
        values = x_ref[:, part].astype(F32)
        _, _, query, keyed, valued = project(values, mean_ref, scaling_ref, params_ref[:, part])
        probs = probabilities(query, keyed, bias_ref).astype(BF16)
        out_ref[:, part] = (values + dot(probs, valued, ((1,), (0,)))).astype(BF16)


def backward_kernel(
    stats_ref, docs_ref, params_ref, x_ref, g_ref, unit_ref, sums_ref, section_ref,
    mean_ref, scaling_ref, bias_ref, sum_ref, cross_ref,
):
    step = pl.program_id(0)

    @pl.when(step == 0)
    def _():
        prepare(STASH, stats_ref, docs_ref, mean_ref, scaling_ref, bias_ref)
        sum_ref[...] = jnp.zeros_like(sum_ref)
        cross_ref[...] = jnp.zeros_like(cross_ref)

    for i in range(x_ref.shape[1] // HEAD):
        part = slice(i * HEAD, (i + 1) * HEAD)
        params = params_ref[:, part]
        unit, hidden, query, keyed, valued = project(x_ref[:, part].astype(F32), mean_ref, scaling_ref, params)
        probs = probabilities(query, keyed, bias_ref)
        g = g_ref[:, part]
        grad_vals = dot(probs.astype(BF16), g, ((0,), (0,)))
        grad_probs = dot(g, valued, ((1,), (1,)))
        centre = jnp.sum(grad_probs * probs, 1, keepdims=True)
        grad_scores = (probs * (grad_probs - centre)).astype(BF16)
        grad_query = dot(grad_scores, keyed, ((1,), (0,))) * SCALE
        grad_keys = dot(grad_scores, query, ((0,), (0,))) * SCALE
        grad_hidden = grad_query * params[1:2] + grad_keys * params[2:3] + grad_vals
        grad_unit = grad_hidden * params[0:1]
        unit_ref[:, part] = grad_unit
        sum_ref[...] += grad_unit
        cross_ref[...] += grad_unit * unit
        section_ref[0:1, part] = jnp.sum(grad_hidden * unit, 0, keepdims=True)
        section_ref[1:2, part] = jnp.sum(grad_query * hidden, 0, keepdims=True)
        section_ref[2:3, part] = jnp.sum(grad_keys * hidden, 0, keepdims=True)

    @pl.when(step == pl.num_programs(0) - 1)
    def _():
        sums_ref[...] = as_rows(
            jnp.sum(sum_ref[...], 1, keepdims=True), jnp.sum(cross_ref[...], 1, keepdims=True)
        )


def result_kernel(stats_ref, sums_ref, x_ref, g_ref, unit_ref, out_ref):
    mean, scaling = mean_and_scaling(stats_ref, STASH)
    mean_grad, mean_cross = as_columns(sums_ref[0:1] / D, sums_ref[1:2] / D)
    for i in range(x_ref.shape[1] // HEAD):
        part = slice(i * HEAD, (i + 1) * HEAD)
        unit = (x_ref[:, part].astype(F32) - mean) * scaling
        inner = unit_ref[:, part] - mean_grad - unit * mean_cross
        out_ref[:, part] = (scaling * inner + g_ref[:, part].astype(F32)).astype(BF16)


def whole(shape):
    return pl.BlockSpec(shape, lambda i: (0, 0))


def columns(rows, heads):
    return pl.BlockSpec((rows, heads * HEAD), lambda i: (0, i))


def forward_layer(stats, docs, params, block, heads=2):
    return pl.pallas_call(
        forward_kernel,
        grid=(HEADS // heads,),
        in_specs=[whole((32, TOK)), whole((1, TOK)), columns(3, heads), columns(TOK, heads)],
        out_specs=columns(TOK, heads),
        out_shape=jax.ShapeDtypeStruct((TOK, WIDTH), BF16),
        scratch_shapes=[pltpu.VMEM((TOK, HEAD), F32)] * 2 + [pltpu.VMEM((TOK, TOK), F32)],
        cost_estimate=pl.CostEstimate(
            flops=4 * HEADS * TOK * TOK * HEAD, bytes_accessed=4 * TOK * WIDTH, transcendentals=HEADS * TOK * TOK
        ),
        compiler_params=pltpu.CompilerParams(vmem_limit_bytes=24 * 2**20),
        name="forward_layer",
    )(stats, docs, params, block)


def backward_layer(stats, docs, params, block, upstream, heads=2):
    return pl.pallas_call(
        backward_kernel,
        grid=(HEADS // heads,),
        in_specs=[whole((32, TOK)), whole((1, TOK)), columns(3, heads), columns(TOK, heads), columns(TOK, heads)],
        out_specs=[columns(TOK, heads), whole((8, TOK)), columns(3, heads)],
        out_shape=[
            jax.ShapeDtypeStruct((TOK, WIDTH), F32),
            jax.ShapeDtypeStruct((8, TOK), F32),
            jax.ShapeDtypeStruct((3, WIDTH), F32),
        ],
        scratch_shapes=[pltpu.VMEM((TOK, HEAD), F32)] * 2
        + [pltpu.VMEM((TOK, TOK), F32)]
        + [pltpu.VMEM((TOK, HEAD), F32)] * 2,
        cost_estimate=pl.CostEstimate(
            flops=10 * HEADS * TOK * TOK * HEAD, bytes_accessed=8 * TOK * WIDTH, transcendentals=HEADS * TOK * TOK
        ),
        compiler_params=pltpu.CompilerParams(vmem_limit_bytes=24 * 2**20),
        name="backward_layer",
    )(stats, docs, params, block, upstream)


def result_layer(stats, sums, block, upstream, grad_unit, heads=3):
    return pl.pallas_call(
        result_kernel,
        grid=(HEADS // heads,),
        in_specs=[whole((32, TOK)), whole((8, TOK))] + [columns(TOK, heads)] * 3,
        out_specs=columns(TOK, heads),
        out_shape=jax.ShapeDtypeStruct((TOK, WIDTH), BF16),
        cost_estimate=pl.CostEstimate(flops=8 * TOK * WIDTH, bytes_accessed=10 * TOK * WIDTH, transcendentals=0),
        compiler_params=pltpu.CompilerParams(vmem_limit_bytes=24 * 2**20),
        name="result_layer",
    )(stats, sums, block, upstream, grad_unit)


def local(sent_act, sent_grad, evicted, layer_params, doc_ids):
    act, grad, stash = sent_act[0, 0], sent_grad[0, 0], evicted[0, 0]
    params, docs = layer_params[0], doc_ids[0, 0]
    place = lax.axis_index("tensor").astype(jnp.int32).reshape(1)

    bwd_in = move(stash, lambda j: 15 - j)
    up_grad = move(grad, lambda j: j - 1)
    fwd_in = move(act, lambda j: j + 1)
    stats = lax.psum(local_stats(place, act, stash), "tensor")
    bwd_stats = move(stats, lambda j: 15 - j)
    fwd_stats = move(stats, lambda j: j + 1)
    kept_input = move(act, lambda j: 14 - j)

    new_act = forward_layer(fwd_stats, docs[0:1], params, fwd_in)
    grad_unit, sums, section_grad = backward_layer(bwd_stats, docs[1:2], params, bwd_in, up_grad)
    sums = lax.psum(sums, "tensor")
    new_grad = result_layer(bwd_stats, sums, bwd_in, up_grad, grad_unit)
    summed = jnp.sum(lax.all_gather(section_grad, "dp"), 0)
    return (new_act[None, None], new_grad[None, None], kept_input[None, None], summed[None])


def solution(mesh):
    blocks = P("dp", "pipe", None, "tensor")
    weights = P("pipe", None, "tensor")
    return jax.shard_map(
        local,
        mesh=mesh,
        in_specs=(blocks, blocks, blocks, weights, P("dp", "pipe", None, None)),
        out_specs=(blocks, blocks, blocks, weights),
        check_vma=False,
    )
```

time: 218 us -> 150 us (0.69)
  waiting for transfers between devices: 66.9 us -> 43.5 us
  Pallas kernels: 0 us -> 20.3 us
  matrix products: 20.2 us -> 0 us
  starting transfers between devices: 42.1 us -> 28.4 us
  blocking collectives: 60 us -> 46.9 us
  other arithmetic: 10.2 us -> 0.02 us
  local copies, waits for them, and re-layouts: 16.9 us -> 8.1 us
    all_to_all x4 -> x0, starting transfers between devices: 31.9 us -> none  [the longest x2 20.1 us: spread_mirror(): lax.all_to_all(trail_parts, 'pipe', split_axis=0, concat_axis=0, tiled=True)]
    all_to_all x4 -> x0, waiting for transfers between devices: 31.4 us -> none  [the longest x2 20 us: spread_mirror(): lax.all_to_all(lead_parts, 'pipe', split_axis=0, concat_axis=0, tiled=True)]
    pallas_call x0 -> x4, Pallas kernels: none -> 20.3 us  [the longest x1 10.1 us: backward_layer(): pl.pallas_call(backward_kernel, grid=(HEADS // heads,), in_specs=[whole((...]
    psum x4 -> x2, blocking collectives: 60 us -> 40.3 us  [the longest x1 26.2 us: local(): stats = lax.psum(local_stats(place, act, stash), 'tensor')]
    ppermute x2 -> x6, starting transfers between devices: 10.1 us -> 28.4 us  [move(): lax.ppermute(block, 'pipe', [(j, route(j) % count) for j in range(count)])]
    dot_general x5 -> x0, matrix products: 11.7 us -> none  [the longest x1 4.07 us: backward_layer(): jnp.einsum('hts,thd->shd', probs.astype(jnp.bfloat16), upper, preferred_e...]
    convert_element_type x5 -> x0, other arithmetic: 8.99 us -> none  [the longest x2 6.8 us: project(): keyed = (hidden * params[2]).astype(jnp.bfloat16).reshape(count, -1, HEAD)]
    sub x2 -> x0, matrix products: 8.52 us -> none  [probabilities(): weights = jnp.exp(scores - peak)]
  transfers between devices with their start and end apart: 6 -> 6, of which waited for: 3 -> 1; matrix products, arithmetic and copies ran while one was open for 20% -> 0% of each run, Pallas kernels for 0% -> 9%
where the time goes in v1:
time: 150 us; the launch traced here: 148 us
  blocking collectives  46.9 us (31%)
  waiting for transfers between devices  43.5 us (29%)
  starting transfers between devices  28.4 us (19%)
  Pallas kernels  20.3 us (14%)
  local copies, waits for them, and re-layouts  8.1 us (5%)
    ppermute x6, waiting for transfers between devices, move(): lax.ppermute(block, 'pipe', [(j, route(j) % count) for j in range(count)])  43.5 us
    ppermute x6, starting transfers between devices, move(): lax.ppermute(block, 'pipe', [(j, route(j) % count) for j in range(count)])  28.4 us
    psum x1, blocking collectives, local(): stats = lax.psum(local_stats(place, act, stash), 'tensor')  26.2 us
    psum x1, blocking collectives, local(): sums = lax.psum(sums, 'tensor')  14.1 us
    pallas_call x1, Pallas kernels, backward_layer(): pl.pallas_call(backward_kernel, grid=(HEADS // heads,), in_specs=[whole((...  10.1 us
    unnamed x16, local copies, waits for them, and re-layouts  7.47 us
    pallas_call x1, Pallas kernels, forward_layer(): pl.pallas_call(forward_kernel, grid=(HEADS // heads,), in_specs=[whole((3...  6.63 us
    all_gather x1, blocking collectives, local(): summed = jnp.sum(lax.all_gather(section_grad, 'dp'), 0)  6.56 us
  transfers between devices with their start and end apart: 6, of which 1 were waited for; matrix products, arithmetic and copies ran while one was open for 0% of the time, Pallas kernels for 9%

profile of v1, /device:TPU:1, one launch (start us, length us, event | category | flops | bytes accessed | tf_op | source)
XLA Modules:
  0.0 148.0 jit_solution(12899540458503240452)
XLA Ops:
  0.6 0.0 copy-start.6
  0.6 14.0 %collective-permute-start.3 = (bf16[256,1536]{1,0:T(8,128)(2,1)}, bf16[256,1536]{1,0:T(8,128)(2,1)S(1)}, u32[]{:S(2)}, u32[]{:S(2)}) collective-permute-start(bf16[256,1536]{1,0:T(8,128)(2,1)} %bitcast.15), channel_id=1, source_target_pairs={{0,480},{32,448},{64,416},{96,384},{128,352},{160,320},{192,288},{... | collective-permute-start | bytes 2359304 | tf_op jit(solution)/shard_map/ppermute | solution.py:23
  14.6 1.9 %collective-permute-start.4 = (bf16[256,1536]{1,0:T(8,128)(2,1)}, bf16[256,1536]{1,0:T(8,128)(2,1)S(1)}, u32[]{:S(2)}, u32[]{:S(2)}) collective-permute-start(bf16[256,1536]{1,0:T(8,128)(2,1)} %bitcast.25), channel_id=1, source_target_pairs={{0,480},{32,0},{64,32},{96,64},{128,96},{160,128},{192,160},{224,1... | collective-permute-start | bytes 2359304 | tf_op jit(solution)/shard_map/ppermute | solution.py:23
  16.5 2.2 %collective-permute-start.5 = (bf16[256,1536]{1,0:T(8,128)(2,1)}, bf16[256,1536]{1,0:T(8,128)(2,1)}, u32[]{:S(2)}, u32[]{:S(2)}) collective-permute-start(bf16[256,1536]{1,0:T(8,128)(2,1)} %bitcast.17), channel_id=1, source_target_pairs={{0,448},{32,416},{64,384},{96,352},{128,320},{160,288},{192,256},{... | collective-permute-start | bytes 2359304 | tf_op jit(solution)/shard_map/ppermute | solution.py:23
  18.7 3.1 %collective-permute-start.1 = (bf16[256,1536]{1,0:T(8,128)(2,1)}, bf16[256,1536]{1,0:T(8,128)(2,1)S(1)}, u32[]{:S(2)}, u32[]{:S(2)}) collective-permute-start(bf16[256,1536]{1,0:T(8,128)(2,1)} %bitcast.18), channel_id=1, source_target_pairs={{0,32},{32,64},{64,96},{96,128},{128,160},{160,192},{192,224},{224... | collective-permute-start | bytes 2359304 | tf_op jit(solution)/shard_map/ppermute | solution.py:23
  21.8 0.0 copy-start
  21.8 1.1 copy-done
  23.0 0.0 copy-start.1
  23.0 1.1 copy-done.1
  24.1 0.0 copy-start.5
  24.1 0.8 local_stats.1
  24.9 26.2 %psum.14 = f32[32,256]{1,0:T(8,128)S(1)} all-reduce(f32[32,256]{1,0:T(8,128)S(1)} %local_stats.1), channel_id=1, replica_groups=mesh['pipe'=16,'tensor'=8,'dp'=4] {'tensor'}, use_global_device_ids=true, to_apply=%region_0.0 | all-reduce | flops 8192 | bytes 65536 | tf_op jit(solution)/shard_map/psum | solution.py:234
  51.1 5.3 %collective-permute-start.2 = (f32[32,256]{1,0:T(8,128)S(1)}, f32[32,256]{1,0:T(8,128)S(1)}, u32[]{:S(2)}, u32[]{:S(2)}) collective-permute-start(f32[32,256]{1,0:T(8,128)S(1)} %psum.14), channel_id=1, source_target_pairs={{0,480},{32,448},{64,416},{96,384},{128,352},{160,320},{192,288},{... | collective-permute-start | bytes 98312 | tf_op jit(solution)/shard_map/ppermute | solution.py:23
  56.4 0.0 copy-done.6
  56.4 0.0 copy-done.5
  56.4 43.5 %collective-permute-done.2.stats_ref = f32[32,256]{1,0:T(8,128)S(1)} collective-permute-done((f32[32,256]{1,0:T(8,128)S(1)}, f32[32,256]{1,0:T(8,128)S(1)}, u32[]{:S(2)}, u32[]{:S(2)}) %collective-permute-start.2) | collective-permute-done | bytes 32800 | tf_op jit(solution)/shard_map/ppermute | solution.py:23
  100.0 1.9 %collective-permute-start = (f32[32,256]{1,0:T(8,128)S(1)}, f32[32,256]{1,0:T(8,128)S(1)}, u32[]{:S(2)}, u32[]{:S(2)}) collective-permute-start(f32[32,256]{1,0:T(8,128)S(1)} %psum.14), channel_id=1, source_target_pairs={{0,32},{32,64},{64,96},{96,128},{128,160},{160,192},{192,224},{224... | collective-permute-start | bytes 98312 | tf_op jit(solution)/shard_map/ppermute | solution.py:23
  101.9 0.0 collective-permute-done.3.x_ref
  101.9 0.0 collective-permute-done.4.g_ref
  101.9 0.0 copy-start.2
  101.9 0.9 copy-done.2
  102.8 0.0 copy-start.3
  102.8 1.1 copy-done.3
  103.9 10.1 %backward_layer.1 = (f32[256,1536]{1,0:T(8,128)S(1)}, f32[8,256]{1,0:T(8,128)S(1)}, f32[3,1536]{1,0:T(4,128)S(1)}) custom-call(f32[32,256]{1,0:T(8,128)S(1)} %collective-permute-done.2.stats_ref, s32[1,256]{1,0:T(1,128)S(1)} %get-tuple-element.10.docs_ref, f32[3,1536]{1,0:T(4,128)S(1)} %bitcast.20, bf16[256,1536]{1,0:T(8,128)(2,1)S(1)} %collective-permute-done.3.x_ref, ...), custom_call_target="tpu_custom_call" | custom-call | flops 1006632960 | bytes 3145728 | tf_op jit(solution)/shard_map/backward_layer/pallas_call | solution.py:192
  114.0 6.6 %all-gather.1 = f32[4,3,1536]{2,1,0:T(4,128)S(1)} all-gather(f32[1,3,1536]{2,1,0:T(4,128)S(1)} %bitcast.22), channel_id=2, replica_groups=mesh['pipe'=16,'tensor'=8,'dp'=4] {'dp'}, dimensions={0}, use_global_device_ids=true | all-gather | bytes 92160 | tf_op jit(solution)/shard_map/all_gather | solution.py:243
  120.6 0.6 broadcast_in_dim.15
  121.2 0.0 collective-permute-done.5
  121.2 14.1 %psum.15.sums_ref = f32[8,256]{1,0:T(8,128)S(1)} all-reduce(f32[8,256]{1,0:T(8,128)S(1)} %get-tuple-element.7), channel_id=1, replica_groups=mesh['pipe'=16,'tensor'=8,'dp'=4] {'tensor'}, use_global_device_ids=true, to_apply=%region_1.0 | all-reduce | flops 2048 | bytes 16384 | tf_op jit(solution)/shard_map/psum | solution.py:241
  135.3 0.0 copy-start.4
  135.3 1.1 copy-done.4
  136.5 2.8 %result_layer.1 = bf16[256,1536]{1,0:T(8,128)(2,1)} custom-call(f32[32,256]{1,0:T(8,128)S(1)} %collective-permute-done.2.stats_ref, f32[8,256]{1,0:T(8,128)S(1)} %psum.15.sums_ref, bf16[256,1536]{1,0:T(8,128)(2,1)S(1)} %collective-permute-done.3.x_ref, bf16[256,1536]{1,0:T(8,128)(2,1)S(1)} %copy-done.4, f32[256,1536]{1,0:T(8,128)S(1)} %get-tuple-element.8.unit_ref), custom_call_target="tpu_custom_call" | custom-call | flops 3145728 | bytes 3932160 | tf_op jit(solution)/shard_map/result_layer/pallas_call | solution.py:214
  139.3 0.0 collective-permute-done.stats_ref
  139.3 0.0 collective-permute-done.1.x_ref
  139.3 6.6 %forward_layer.1 = bf16[256,1536]{1,0:T(8,128)(2,1)} custom-call(f32[32,256]{1,0:T(8,128)S(1)} %collective-permute-done.stats_ref, s32[1,256]{1,0:T(1,128)S(1)} %get-tuple-element.11.docs_ref, f32[3,1536]{1,0:T(4,128)S(1)} %bitcast.21, bf16[256,1536]{1,0:T(8,128)(2,1)S(1)} %collective-permute-done.1.x_ref), custom_call_target="tpu_custom_call" | custom-call | flops 402653184 | bytes 1572864 | tf_op jit(solution)/shard_map/forward_layer/pallas_call | solution.py:176
  145.9 2.1 %copy.13 = bf16[1,1,256,1536]{3,2,1,0:T(8,128)(2,1)} copy(bf16[1,1,256,1536]{3,2,1,0:T(8,128)(2,1)} %bitcast.8) | data formatting | bytes 1572864
  (3 shorter events, 0.0 us)
Async XLA Ops:
  0.6 55.8 %copy-start.6 = (s32[1,1,2,256]{3,2,1,0:T(2,128)S(1)}, s32[1,1,2,256]{3,2,1,0:T(2,128)}, u32[]{:S(2)}) copy-start(s32[1,1,2,256]{3,2,1,0:T(2,128)} %param.9) | copy-start | bytes 6148
  0.6 101.2 %collective-permute-start.3 = (bf16[256,1536]{1,0:T(8,128)(2,1)}, bf16[256,1536]{1,0:T(8,128)(2,1)S(1)}, u32[]{:S(2)}, u32[]{:S(2)}) collective-permute-start(bf16[256,1536]{1,0:T(8,128)(2,1)} %bitcast.15), channel_id=1, source_target_pairs={{0,480},{32,448},{64,416},{96,384},{128,352},{160,320},{192,288},{... | collective-permute-start | bytes 2359304 | tf_op jit(solution)/shard_map/ppermute | solution.py:23
  14.6 87.3 %collective-permute-start.4 = (bf16[256,1536]{1,0:T(8,128)(2,1)}, bf16[256,1536]{1,0:T(8,128)(2,1)S(1)}, u32[]{:S(2)}, u32[]{:S(2)}) collective-permute-start(bf16[256,1536]{1,0:T(8,128)(2,1)} %bitcast.25), channel_id=1, source_target_pairs={{0,480},{32,0},{64,32},{96,64},{128,96},{160,128},{192,160},{224,1... | collective-permute-start | bytes 2359304 | tf_op jit(solution)/shard_map/ppermute | solution.py:23
  16.5 104.7 %collective-permute-start.5 = (bf16[256,1536]{1,0:T(8,128)(2,1)}, bf16[256,1536]{1,0:T(8,128)(2,1)}, u32[]{:S(2)}, u32[]{:S(2)}) collective-permute-start(bf16[256,1536]{1,0:T(8,128)(2,1)} %bitcast.17), channel_id=1, source_target_pairs={{0,448},{32,416},{64,384},{96,352},{128,320},{160,288},{192,256},{... | collective-permute-start | bytes 2359304 | tf_op jit(solution)/shard_map/ppermute | solution.py:23
  18.7 120.6 %collective-permute-start.1 = (bf16[256,1536]{1,0:T(8,128)(2,1)}, bf16[256,1536]{1,0:T(8,128)(2,1)S(1)}, u32[]{:S(2)}, u32[]{:S(2)}) collective-permute-start(bf16[256,1536]{1,0:T(8,128)(2,1)} %bitcast.18), channel_id=1, source_target_pairs={{0,32},{32,64},{64,96},{96,128},{128,160},{160,192},{192,224},{224... | collective-permute-start | bytes 2359304 | tf_op jit(solution)/shard_map/ppermute | solution.py:23
  21.8 1.1 copy-start
  23.0 1.1 copy-start.1
  24.1 32.3 %copy-start.5 = (f32[1,3,1536]{2,0,1:T(1,128)S(1)}, f32[1,3,1536]{2,0,1:T(1,128)}, u32[]{:S(2)}) copy-start(f32[1,3,1536]{2,0,1:T(1,128)} %param.8) | copy-start | bytes 55300
  51.1 48.9 %collective-permute-start.2 = (f32[32,256]{1,0:T(8,128)S(1)}, f32[32,256]{1,0:T(8,128)S(1)}, u32[]{:S(2)}, u32[]{:S(2)}) collective-permute-start(f32[32,256]{1,0:T(8,128)S(1)} %psum.14), channel_id=1, source_target_pairs={{0,480},{32,448},{64,416},{96,384},{128,352},{160,320},{192,288},{... | collective-permute-start | bytes 98312 | tf_op jit(solution)/shard_map/ppermute | solution.py:23
  100.0 39.3 %collective-permute-start = (f32[32,256]{1,0:T(8,128)S(1)}, f32[32,256]{1,0:T(8,128)S(1)}, u32[]{:S(2)}, u32[]{:S(2)}) collective-permute-start(f32[32,256]{1,0:T(8,128)S(1)} %psum.14), channel_id=1, source_target_pairs={{0,32},{32,64},{64,96},{96,128},{128,160},{160,192},{192,224},{224... | collective-permute-start | bytes 98312 | tf_op jit(solution)/shard_map/ppermute | solution.py:23
  101.9 0.9 copy-start.2
  102.8 1.1 copy-start.3
  135.3 1.1 copy-start.4

commit v2 on v1

v2 whole, which is shorter than its diff:
```python
import functools

import jax
import jax.numpy as jnp
from jax import lax
from jax.experimental import pallas as pl
from jax.experimental.pallas import tpu as pltpu
from jax.sharding import PartitionSpec as P

D = 12288
HEAD = 128
TOK = 256
N_TENSOR = 8
WIDTH = D // N_TENSOR
HEADS = WIDTH // HEAD
SCALE = HEAD ** (-0.5)
EPS = 1e-05
LOG2E = 1.4426950408889634
PIECES = 4
SUM, SQUARES, CROSS, GRAD = 0, 1, 2, 3
F32 = jnp.float32
BF16 = jnp.bfloat16
VMEM = 56 * 2**20


def move(block, route):
    count = lax.axis_size("pipe")
    pairs = [(j, route(j) % count) for j in range(count) if route(j) is not None]
    return lax.ppermute(block, "pipe", pairs)


def dot(left, right, dims):
    return lax.dot_general(left, right, (dims, ((), ())), preferred_element_type=F32)


def as_rows(*columns):
    lane = lax.broadcasted_iota(jnp.int32, (TOK, HEAD), 1)
    packed = jnp.broadcast_to(columns[-1], (TOK, HEAD))
    for i in range(len(columns) - 2, -1, -1):
        packed = jnp.where(lane <= i, columns[i], packed)
    return jnp.transpose(packed)[0:8]


def as_columns(first, second):
    row = lax.broadcasted_iota(jnp.int32, (HEAD, TOK), 0)
    both = jnp.transpose(jnp.where(row == 0, first, second))
    return both[:, 0:1], both[:, 1:2]


def to_all(out_ref, rows):
    for i in range(N_TENSOR):
        out_ref[8 * i:8 * i + 8] = rows


def from_all(ref, row):
    return [ref[8 * i + row:8 * i + row + 1] for i in range(N_TENSOR)]


class Spread:
    def __init__(self, pivot_ref, sum_ref, square_ref):
        self.pivot, self.sum, self.square = pivot_ref, sum_ref, square_ref

    def first(self, piece):
        self.pivot[...] = jnp.broadcast_to(jnp.sum(piece, 1, keepdims=True) / HEAD, (TOK, HEAD))
        self.sum[...] = jnp.zeros_like(self.sum)
        self.square[...] = jnp.zeros_like(self.square)

    def add(self, piece):
        away = piece - self.pivot[...]
        self.sum[...] += away
        self.square[...] += away * away

    def result(self):
        away = jnp.sum(self.sum[...], 1, keepdims=True)
        square = jnp.sum(self.square[...], 1, keepdims=True)
        return away + WIDTH * self.pivot[:, 0:1], square - away * away / WIDTH


def stats_kernel(*refs):
    pieces, out_ref, scratch = refs[:PIECES], refs[PIECES], refs[PIECES + 1:]
    spread = Spread(*scratch)
    spread.first(pieces[0][:, 0:HEAD].astype(F32))
    for ref in pieces:
        for i in range(ref.shape[1] // HEAD):
            spread.add(ref[:, i * HEAD:(i + 1) * HEAD].astype(F32))
    to_all(out_ref, as_rows(*spread.result()))


def local_stats(block):
    pieces = [pl.BlockSpec((TOK, WIDTH // PIECES), functools.partial(lambda p, i: (0, p), p)) for p in range(PIECES)]
    return pl.pallas_call(
        stats_kernel,
        grid=(1,),
        in_specs=pieces,
        out_specs=whole((64, TOK)),
        out_shape=jax.ShapeDtypeStruct((8 * N_TENSOR, TOK), F32),
        scratch_shapes=[pltpu.VMEM((TOK, HEAD), F32)] * 3,
        cost_estimate=pl.CostEstimate(flops=8 * TOK * WIDTH, bytes_accessed=2 * TOK * WIDTH, transcendentals=0),
        compiler_params=pltpu.CompilerParams(vmem_limit_bytes=VMEM),
        name="local_stats",
    )(*[block] * PIECES)


def exchange(rows):
    return lax.all_to_all(rows, "tensor", 0, 0, tiled=True)


def mean_and_scaling(stats_ref):
    sums, squares = from_all(stats_ref, SUM), from_all(stats_ref, SQUARES)
    mean = sum(sums) / D
    apart = [piece / WIDTH - mean for piece in sums]
    spread = (sum(squares) + WIDTH * sum(piece * piece for piece in apart)) / D
    return as_columns(mean, lax.rsqrt(spread + EPS))


def prepare(which, stats_ref, docs_ref, mean_ref, scaling_ref, bias_ref):
    mean, scaling = mean_and_scaling(stats_ref)
    mean_ref[...] = jnp.broadcast_to(mean, (TOK, HEAD))
    scaling_ref[...] = jnp.broadcast_to(scaling, (TOK, HEAD))
    docs = docs_ref[which:which + 1].astype(F32)
    column, _ = as_columns(docs, docs)
    t = lax.broadcasted_iota(jnp.int32, (TOK, TOK), 0)
    u = lax.broadcasted_iota(jnp.int32, (TOK, TOK), 1)
    bias_ref[...] = jnp.where((t <= u) & (column == docs), 0.0, -1e30)


def project(values, mean_ref, scaling_ref, params):
    unit = (values - mean_ref[...]) * scaling_ref[...]
    hidden = unit * params[0]
    query = (hidden * params[1]).astype(BF16)
    keyed = (hidden * params[2]).astype(BF16)
    return unit, hidden, query, keyed, hidden.astype(BF16)


def probabilities(query, keyed, bias_ref):
    scores = dot(keyed, query, ((1,), (1,))) * (SCALE * LOG2E) + bias_ref[...]
    weights = jnp.exp2(scores - jnp.max(scores, 0, keepdims=True))
    return weights * (1.0 / jnp.sum(weights, 0, keepdims=True))


def backward_kernel(
    odd_ref, stats_ref, docs_ref, params_ref, x_ref, one_ref, two_ref,
    unit_ref, act_ref, g_ref, sums_ref, section_ref,
    mean_ref, scaling_ref, bias_ref, sum_ref, cross_ref, *scratch
):
    step = pl.program_id(0)
    spread = Spread(*scratch)

    @pl.when(odd_ref[0] == 0)
    def _():
        act_ref[...] = one_ref[...]
        g_ref[...] = two_ref[...]

    @pl.when(odd_ref[0] == 1)
    def _():
        act_ref[...] = two_ref[...]
        g_ref[...] = one_ref[...]

    @pl.when(step == 0)
    def _():
        prepare(1, stats_ref, docs_ref, mean_ref, scaling_ref, bias_ref)
        sum_ref[...] = jnp.zeros_like(sum_ref)
        cross_ref[...] = jnp.zeros_like(cross_ref)
        spread.first(act_ref[:, 0:HEAD].astype(F32))

    for i in range(x_ref.shape[1] // HEAD):
        part = slice(i * HEAD, (i + 1) * HEAD)
        spread.add(act_ref[:, part].astype(F32))
        params = params_ref[:, :, part]
        unit, hidden, query, keyed, valued = project(x_ref[:, part].astype(F32), mean_ref, scaling_ref, params)
        probs = probabilities(query, keyed, bias_ref)
        g = g_ref[:, part]
        grad_vals = dot(probs.astype(BF16), g, ((1,), (0,)))
        grad_probs = dot(valued, g, ((1,), (1,)))
        centre = jnp.sum(grad_probs * probs, 0, keepdims=True)
        grad_scores = (probs * (grad_probs - centre)).astype(BF16)
        grad_query = dot(grad_scores, keyed, ((0,), (0,)))
        grad_keys = dot(grad_scores, query, ((1,), (0,)))
        grad_hidden = grad_query * (params[1] * SCALE) + grad_keys * (params[2] * SCALE) + grad_vals
        grad_unit = grad_hidden * params[0]
        unit_ref[:, part] = grad_unit
        sum_ref[...] += grad_unit
        cross_ref[...] += grad_unit * unit
        section_ref[0, :, part] = jnp.sum(grad_hidden * unit, 0, keepdims=True)
        section_ref[1, :, part] = jnp.sum(grad_query * hidden, 0, keepdims=True) * SCALE
        section_ref[2, :, part] = jnp.sum(grad_keys * hidden, 0, keepdims=True) * SCALE

    @pl.when(step == pl.num_programs(0) - 1)
    def _():
        total, squares = spread.result()
        grad = jnp.sum(sum_ref[...], 1, keepdims=True)
        cross = jnp.sum(cross_ref[...], 1, keepdims=True)
        to_all(sums_ref, as_rows(total, squares, cross, grad))


def finish_kernel(
    stats_ref, sums_ref, docs_ref, params_ref, act_ref, x_ref, g_ref, unit_ref, new_act_ref, new_grad_ref,
    mean_ref, scaling_ref, bias_ref, own_ref,
):
    @pl.when(pl.program_id(0) == 0)
    def _():
        prepare(0, sums_ref, docs_ref, mean_ref, scaling_ref, bias_ref)
        mean, scaling = mean_and_scaling(stats_ref)
        mean_grad, mean_cross = as_columns(
            sum(from_all(sums_ref, GRAD)) / D, sum(from_all(sums_ref, CROSS)) / D
        )
        for i, column in enumerate((mean, scaling, mean_grad, mean_cross)):
            own_ref[i] = jnp.broadcast_to(column, (TOK, HEAD))

    for i in range(x_ref.shape[1] // HEAD):
        part = slice(i * HEAD, (i + 1) * HEAD)
        unit = (x_ref[:, part].astype(F32) - own_ref[0]) * own_ref[1]
        inner = unit_ref[:, part] - own_ref[2] - unit * own_ref[3]
        new_grad_ref[:, part] = (own_ref[1] * inner + g_ref[:, part].astype(F32)).astype(BF16)
        values = act_ref[:, part].astype(F32)
        _, _, query, keyed, valued = project(values, mean_ref, scaling_ref, params_ref[:, :, part])
        probs = probabilities(query, keyed, bias_ref).astype(BF16)
        new_act_ref[:, part] = (values + dot(probs, valued, ((0,), (0,)))).astype(BF16)


def whole(shape):
    return pl.BlockSpec(shape, lambda i: (0, 0))


def columns(rows, heads):
    return pl.BlockSpec((rows, heads * HEAD), lambda i: (0, i))


def layer(heads):
    return pl.BlockSpec((3, 1, heads * HEAD), lambda i: (0, 0, i))


def backward_layer(odd, stats, docs, params, block, one, two, heads=12):
    wide = columns(TOK, heads)
    return pl.pallas_call(
        backward_kernel,
        grid=(HEADS // heads,),
        in_specs=[pl.BlockSpec(memory_space=pltpu.SMEM), whole((64, TOK)), whole((2, TOK)), layer(heads)] + [wide] * 3,
        out_specs=[wide, wide, wide, whole((64, TOK)), layer(heads)],
        out_shape=[
            jax.ShapeDtypeStruct((TOK, WIDTH), F32),
            jax.ShapeDtypeStruct((TOK, WIDTH), BF16),
            jax.ShapeDtypeStruct((TOK, WIDTH), BF16),
            jax.ShapeDtypeStruct((64, TOK), F32),
            jax.ShapeDtypeStruct((3, 1, WIDTH), F32),
        ],
        scratch_shapes=[pltpu.VMEM((TOK, HEAD), F32)] * 2
        + [pltpu.VMEM((TOK, TOK), F32)]
        + [pltpu.VMEM((TOK, HEAD), F32)] * 5,
        cost_estimate=pl.CostEstimate(
            flops=10 * HEADS * TOK * TOK * HEAD, bytes_accessed=14 * TOK * WIDTH, transcendentals=HEADS * TOK * TOK
        ),
        compiler_params=pltpu.CompilerParams(vmem_limit_bytes=VMEM),
        name="backward_layer",
    )(odd, stats, docs, params, block, one, two)


def finish_layer(stats, sums, docs, params, act, block, upstream, grad_unit, heads=12):
    wide = columns(TOK, heads)
    return pl.pallas_call(
        finish_kernel,
        grid=(HEADS // heads,),
        in_specs=[whole((64, TOK)), whole((64, TOK)), whole((2, TOK)), layer(heads)] + [wide] * 4,
        out_specs=[wide, wide],
        out_shape=[jax.ShapeDtypeStruct((TOK, WIDTH), BF16)] * 2,
        scratch_shapes=[pltpu.VMEM((TOK, HEAD), F32)] * 2
        + [pltpu.VMEM((TOK, TOK), F32), pltpu.VMEM((4, TOK, HEAD), F32)],
        cost_estimate=pl.CostEstimate(
            flops=4 * HEADS * TOK * TOK * HEAD, bytes_accessed=14 * TOK * WIDTH, transcendentals=HEADS * TOK * TOK
        ),
        compiler_params=pltpu.CompilerParams(vmem_limit_bytes=VMEM),
        name="finish_layer",
    )(stats, sums, docs, params, act, block, upstream, grad_unit)


def mirror(j):
    return 15 - j


def odd_swap(j):
    return j + 1 if j % 2 else j - 1


def even_swap(j):
    return j - 1 if j % 2 else j + 1


def far(wanted):
    return lambda j: 14 - j if (j % 4 == 1) == wanted else None


def local(sent_act, sent_grad, evicted, layer_params, doc_ids):
    act, grad, stash = sent_act[0, 0], sent_grad[0, 0], evicted[0, 0]
    params, docs = jnp.transpose(layer_params, (1, 0, 2)), doc_ids[0, 0]
    place = lax.axis_index("pipe").astype(jnp.int32)
    odd = place & 1

    bwd_in = move(stash, mirror)
    swapped_odd = move(jnp.where(odd == 1, act, grad), odd_swap)
    swapped_even = move(jnp.where(odd == 1, grad, act), even_swap)

    stats = exchange(local_stats(bwd_in))
    later_act, swapped_odd, swapped_even = lax.optimization_barrier((act, swapped_odd, swapped_even))
    kept_near = move(later_act, far(False))
    grad_unit, fwd_in, up_grad, sums, section_grad = backward_layer(
        odd.reshape(1), stats, docs, params, bwd_in, swapped_odd, swapped_even
    )
    last_act, sums, section_grad = lax.optimization_barrier((act, sums, section_grad))
    kept_far = move(last_act, far(True))
    sums = exchange(sums)
    summed = jnp.transpose(jnp.sum(lax.all_gather(section_grad, "dp"), 0), (1, 0, 2))
    new_act, new_grad = finish_layer(stats, sums, docs, params, fwd_in, bwd_in, up_grad, grad_unit)
    kept_input = jnp.where(place & 3 == 1, kept_far, kept_near)
    return (new_act[None, None], new_grad[None, None], kept_input[None, None], summed)


def solution(mesh):
    blocks = P("dp", "pipe", None, "tensor")
    weights = P("pipe", None, "tensor")
    return jax.shard_map(
        local,
        mesh=mesh,
        in_specs=(blocks, blocks, blocks, weights, P("dp", "pipe", None, None)),
        out_specs=(blocks, blocks, blocks, weights),
        check_vma=False,
    )
```

time: 150 us -> 109 us (0.73)
  the two profiles are of different devices: /device:TPU:1 before, /device:TPU:161 now
where the time goes in v2:
time: 109 us
  starting transfers between devices  50.4 us (46%)
  blocking collectives  17.7 us (16%)
  Pallas kernels  17.4 us (16%)
  waiting for transfers between devices  17.1 us (16%)
  local copies, waits for them, and re-layouts  2.77 us (3%)
  other arithmetic  2.64 us (2%)
    ppermute x5, starting transfers between devices, move(): return lax.ppermute(block, 'pipe', pairs)  37.1 us
    all_gather x1, blocking collectives, local(): lax.all_gather(section_grad, 'dp')  17.7 us
    ppermute x5, waiting for transfers between devices, move(): return lax.ppermute(block, 'pipe', pairs)  17.1 us
    all_to_all x2, starting transfers between devices, exchange(): return lax.all_to_all(rows, 'tensor', 0, 0, tiled=True)  13.3 us
    pallas_call x1, Pallas kernels, backward_layer(): pl.pallas_call(backward_kernel, grid=(HEADS // heads,), in_specs=[pl.Bloc...  8.97 us
    pallas_call x1, Pallas kernels, finish_layer(): pl.pallas_call(finish_kernel, grid=(HEADS // heads,), in_specs=[whole((64...  6.04 us
    pallas_call x1, Pallas kernels, local_stats(): pl.pallas_call(stats_kernel, grid=(1,), in_specs=pieces, out_specs=whole(...  2.43 us
  transfers between devices with their start and end apart: 7, of which 2 were waited for; matrix products, arithmetic and copies ran while one was open for 2% of the time, Pallas kernels for 16%

profile of v2, /device:TPU:161, one launch (start us, length us, event | category | flops | bytes accessed | tf_op | source)
XLA Modules:
  0.0 108.8 jit_solution(1051648046951741073)
XLA Ops:
  0.6 10.4 %collective-permute-start = (bf16[256,1536]{1,0:T(8,128)(2,1)}, bf16[256,1536]{1,0:T(8,128)(2,1)S(1)}, u32[]{:S(2)}, u32[]{:S(2)}) collective-permute-start(bf16[256,1536]{1,0:T(8,128)(2,1)} %bitcast.29), channel_id=1, source_target_pairs={{0,480},{32,448},{64,416},{96,384},{128,352},{160,320},{192,288},{... | collective-permute-start | bytes 2359304 | tf_op jit(solution)/shard_map/ppermute | solution.py:29
  11.0 1.5 %bitcast_select_fusion = (bf16[256,1536]{1,0:T(8,128)(2,1)S(1)}, bf16[256,1536]{1,0:T(8,128)(2,1)S(1)}) fusion(bf16[1,1,256,1536]{3,2,1,0:T(8,128)(2,1)} %param.6, pred[]{:T(512)S(6)} %eq.7, bf16[1,1,256,1536]{3,2,1,0:T(8,128)(2,1)} %param.5), kind=kLoop, calls=%fused_computation | loop fusion | flops 786432 | bytes 3145729 | tf_op jit(solution)/shard_map/jit(_where)/select_n | solution.py:300
  12.5 3.1 %collective-permute-start.1 = (bf16[256,1536]{1,0:T(8,128)(2,1)S(1)}, bf16[256,1536]{1,0:T(8,128)(2,1)}, u32[]{:S(2)}, u32[]{:S(2)}) collective-permute-start(bf16[256,1536]{1,0:T(8,128)(2,1)S(1)} %get-tuple-element.31), channel_id=1, source_target_pairs={{0,480},{32,64},{64,32},{96,128},{128,96},{160,192},{192,160},{224... | collective-permute-start | bytes 2359304 | tf_op jit(solution)/shard_map/ppermute | solution.py:29
  15.6 0.0 copy-start.1
  15.6 2.1 %collective-permute-start.2 = (bf16[256,1536]{1,0:T(8,128)(2,1)S(1)}, bf16[256,1536]{1,0:T(8,128)(2,1)}, u32[]{:S(2)}, u32[]{:S(2)}) collective-permute-start(bf16[256,1536]{1,0:T(8,128)(2,1)S(1)} %get-tuple-element.30), channel_id=1, source_target_pairs={{0,32},{32,0},{64,96},{96,64},{128,160},{160,128},{192,224},{224,1... | collective-permute-start | bytes 2359304 | tf_op jit(solution)/shard_map/ppermute | solution.py:29
  17.7 10.9 %collective-permute-done.refs_0_.refs_1_.refs_2_.refs_3_.x_ref = bf16[256,1536]{1,0:T(8,128)(2,1)S(1)} collective-permute-done((bf16[256,1536]{1,0:T(8,128)(2,1)}, bf16[256,1536]{1,0:T(8,128)(2,1)S(1)}, u32[]{:S(2)}, u32[]{:S(2)}) %collective-permute-start) | collective-permute-done | bytes 786464 | tf_op jit(solution)/shard_map/ppermute | solution.py:29
  28.6 0.0 copy-start
  28.6 0.9 copy-done
  29.5 2.4 %local_stats.1 = f32[64,256]{1,0:T(8,128)} custom-call(bf16[256,1536]{1,0:T(8,128)(2,1)} %copy-done, bf16[256,1536]{1,0:T(8,128)(2,1)} %copy-done, bf16[256,1536]{1,0:T(8,128)(2,1)} %copy-done, bf16[256,1536]{1,0:T(8,128)(2,1)} %copy-done), custom_call_target="tpu_custom_call" | custom-call | flops 3145728 | bytes 786432 | tf_op jit(solution)/shard_map/local_stats/pallas_call | solution.py:91
  31.9 6.6 %all-to-all-start = ((f32[8,8,256]{2,1,0:T(8,128)}), f32[8,8,256]{2,1,0:T(8,128)S(1)}, u32[]{:S(2)}, u32[]{:S(2)}) async-start(f32[8,8,256]{2,1,0:T(8,128)} %bitcast.23), calls=%async_computation | async-start | bytes 131072 | tf_op jit(solution)/shard_map/all_to_all | solution.py:105
  38.5 0.0 collective-permute-done.1.one_ref
  38.5 6.2 %collective-permute-done.2.two_ref = bf16[256,1536]{1,0:T(8,128)(2,1)} collective-permute-done((bf16[256,1536]{1,0:T(8,128)(2,1)S(1)}, bf16[256,1536]{1,0:T(8,128)(2,1)}, u32[]{:S(2)}, u32[]{:S(2)}) %collective-permute-start.2) | collective-permute-done | bytes 786464 | tf_op jit(solution)/shard_map/ppermute | solution.py:29
  44.7 0.0 copy-done.1
  44.7 20.9 %collective-permute-start.4 = (bf16[256,1536]{1,0:T(8,128)(2,1)S(1)}, bf16[256,1536]{1,0:T(8,128)(2,1)S(1)}, u32[]{:S(2)}, u32[]{:S(2)}) collective-permute-start(bf16[256,1536]{1,0:T(8,128)(2,1)S(1)} %bitcast.18), channel_id=1, source_target_pairs={{0,448},{64,384},{96,352},{128,320},{192,256},{224,224},{256,192},... | collective-permute-start | bytes 2359304 | tf_op jit(solution)/shard_map/ppermute | solution.py:29
  65.6 0.0 all-to-all-done
  65.6 0.0 copy-start.2
  65.6 0.6 copy-done.2
  66.2 9.0 %backward_layer.1 = (f32[256,1536]{1,0:T(8,128)}, bf16[256,1536]{1,0:T(8,128)(2,1)}, bf16[256,1536]{1,0:T(8,128)(2,1)}, f32[64,256]{1,0:T(8,128)}, f32[3,1,1536]{2,1,0:T(1,128)}) custom-call(s32[1]{0:T(128)} %bitcast.4.odd_ref, f32[64,256]{1,0:T(8,128)} %bitcast.20, s32[2,256]{1,0:T(2,128)} %bitcast.27, f32[3,1,1536]{2,1,0:T(1,128)} %bitcast.25, ...), custom_call_target="tpu_custom_call" | custom-call | flops 1006632960 | bytes 5505024 | tf_op jit(solution)/shard_map/backward_layer/pallas_call | solution.py:235
  75.2 0.7 collective-permute-start.3
  75.9 6.7 %all-to-all-start.1 = ((f32[8,8,256]{2,1,0:T(8,128)}), f32[8,8,256]{2,1,0:T(8,128)S(1)}, u32[]{:S(2)}, u32[]{:S(2)}) async-start(f32[8,8,256]{2,1,0:T(8,128)} %bitcast.24), calls=%async_computation.1 | async-start | bytes 131072 | tf_op jit(solution)/shard_map/all_to_all | solution.py:105
  82.6 17.7 %all-gather = f32[12,1,1536]{2,1,0:T(1,128)S(1)} all-gather(f32[3,1,1536]{2,1,0:T(1,128)} %get-tuple-element.29), channel_id=2, replica_groups=mesh['pipe'=16,'tensor'=8,'dp'=4] {'dp'}, dimensions={0}, use_global_device_ids=true | all-gather | bytes 92160 | tf_op jit(solution)/shard_map/all_gather | solution.py:311
  100.3 0.2 reduce.2
  100.5 0.6 transpose.7
  101.1 0.0 all-to-all-done.1
  101.1 0.0 copy-start.3
  101.2 0.6 copy-done.3
  101.8 6.0 %finish_layer.1 = (bf16[256,1536]{1,0:T(8,128)(2,1)}, bf16[256,1536]{1,0:T(8,128)(2,1)}) custom-call(f32[64,256]{1,0:T(8,128)} %bitcast.21, f32[64,256]{1,0:T(8,128)} %bitcast.22, s32[2,256]{1,0:T(2,128)} %bitcast.28, f32[3,1,1536]{2,1,0:T(1,128)} %bitcast.26, bf16[256,1536]{1,0:T(8,128)(2,1)} %get-tuple-element.22.act_ref, bf16[256,1536]{1,0:T(8,128)(2,1)} %copy-done, ...), custom_call_target="tpu_custom_call" | custom-call | flops 402653184 | bytes 5505024 | tf_op jit(solution)/shard_map/finish_layer/pallas_call | solution.py:260
  107.8 0.0 collective-permute-done.4
  107.8 0.0 collective-permute-done.3
  107.8 1.0 select_bitcast_fusion
  (2 shorter events, 0.1 us)
Async XLA Ops:
  0.6 27.9 %collective-permute-start = (bf16[256,1536]{1,0:T(8,128)(2,1)}, bf16[256,1536]{1,0:T(8,128)(2,1)S(1)}, u32[]{:S(2)}, u32[]{:S(2)}) collective-permute-start(bf16[256,1536]{1,0:T(8,128)(2,1)} %bitcast.29), channel_id=1, source_target_pairs={{0,480},{32,448},{64,416},{96,384},{128,352},{160,320},{192,288},{... | collective-permute-start | bytes 2359304 | tf_op jit(solution)/shard_map/ppermute | solution.py:29
  12.5 26.0 %collective-permute-start.1 = (bf16[256,1536]{1,0:T(8,128)(2,1)S(1)}, bf16[256,1536]{1,0:T(8,128)(2,1)}, u32[]{:S(2)}, u32[]{:S(2)}) collective-permute-start(bf16[256,1536]{1,0:T(8,128)(2,1)S(1)} %get-tuple-element.31), channel_id=1, source_target_pairs={{0,480},{32,64},{64,32},{96,128},{128,96},{160,192},{192,160},{224... | collective-permute-start | bytes 2359304 | tf_op jit(solution)/shard_map/ppermute | solution.py:29
  15.6 29.1 %copy-start.1 = (bf16[1,1,256,1536]{3,2,1,0:T(8,128)(2,1)S(1)}, bf16[1,1,256,1536]{3,2,1,0:T(8,128)(2,1)}, u32[]{:S(2)}) copy-start(bf16[1,1,256,1536]{3,2,1,0:T(8,128)(2,1)} %param.5) | copy-start | bytes 2359300
  15.6 29.1 %collective-permute-start.2 = (bf16[256,1536]{1,0:T(8,128)(2,1)S(1)}, bf16[256,1536]{1,0:T(8,128)(2,1)}, u32[]{:S(2)}, u32[]{:S(2)}) collective-permute-start(bf16[256,1536]{1,0:T(8,128)(2,1)S(1)} %get-tuple-element.30), channel_id=1, source_target_pairs={{0,32},{32,0},{64,96},{96,64},{128,160},{160,128},{192,224},{224,1... | collective-permute-start | bytes 2359304 | tf_op jit(solution)/shard_map/ppermute | solution.py:29
  28.6 0.9 copy-start
  31.9 33.7 %all-to-all-start = ((f32[8,8,256]{2,1,0:T(8,128)}), f32[8,8,256]{2,1,0:T(8,128)S(1)}, u32[]{:S(2)}, u32[]{:S(2)}) async-start(f32[8,8,256]{2,1,0:T(8,128)} %bitcast.23), calls=%async_computation | async-start | bytes 131072 | tf_op jit(solution)/shard_map/all_to_all | solution.py:105
  44.7 63.1 %collective-permute-start.4 = (bf16[256,1536]{1,0:T(8,128)(2,1)S(1)}, bf16[256,1536]{1,0:T(8,128)(2,1)S(1)}, u32[]{:S(2)}, u32[]{:S(2)}) collective-permute-start(bf16[256,1536]{1,0:T(8,128)(2,1)S(1)} %bitcast.18), channel_id=1, source_target_pairs={{0,448},{64,384},{96,352},{128,320},{192,256},{224,224},{256,192},... | collective-permute-start | bytes 2359304 | tf_op jit(solution)/shard_map/ppermute | solution.py:29
  65.6 0.6 copy-start.2
  75.2 32.6 %collective-permute-start.3 = (bf16[256,1536]{1,0:T(8,128)(2,1)S(1)}, bf16[256,1536]{1,0:T(8,128)(2,1)S(1)}, u32[]{:S(2)}, u32[]{:S(2)}) collective-permute-start(bf16[256,1536]{1,0:T(8,128)(2,1)S(1)} %bitcast.19), channel_id=1, source_target_pairs={{32,416},{160,288},{288,160},{416,32},{33,417},{161,289},{289,161}... | collective-permute-start | bytes 2359304 | tf_op jit(solution)/shard_map/ppermute | solution.py:29
  75.9 25.3 %all-to-all-start.1 = ((f32[8,8,256]{2,1,0:T(8,128)}), f32[8,8,256]{2,1,0:T(8,128)S(1)}, u32[]{:S(2)}, u32[]{:S(2)}) async-start(f32[8,8,256]{2,1,0:T(8,128)} %bitcast.24), calls=%async_computation.1 | async-start | bytes 131072 | tf_op jit(solution)/shard_map/all_to_all | solution.py:105
  101.1 0.6 copy-start.3

commit v3 on v2

--- a/solution.py
+++ b/solution.py
@@ -1,5 +1,3 @@
-import functools
-
 import jax
 import jax.numpy as jnp
 from jax import lax
@@ -9,6 +7,7 @@
 
 D = 12288
 HEAD = 128
+HALF = 128
 TOK = 256
 N_TENSOR = 8
 WIDTH = D // N_TENSOR
@@ -16,7 +15,6 @@
 SCALE = HEAD ** (-0.5)
 EPS = 1e-05
 LOG2E = 1.4426950408889634
-PIECES = 4
 SUM, SQUARES, CROSS, GRAD = 0, 1, 2, 3
 F32 = jnp.float32
 BF16 = jnp.bfloat16
@@ -76,29 +74,25 @@
         return away + WIDTH * self.pivot[:, 0:1], square - away * away / WIDTH
 
 
-def stats_kernel(*refs):
-    pieces, out_ref, scratch = refs[:PIECES], refs[PIECES], refs[PIECES + 1:]
+def stats_kernel(x_ref, out_ref, *scratch):
     spread = Spread(*scratch)
-    spread.first(pieces[0][:, 0:HEAD].astype(F32))
-    for ref in pieces:
-        for i in range(ref.shape[1] // HEAD):
-            spread.add(ref[:, i * HEAD:(i + 1) * HEAD].astype(F32))
+    spread.first(x_ref[:, 0:HEAD].astype(F32))
+    for h in range(HEADS):
+        spread.add(x_ref[:, h * HEAD:(h + 1) * HEAD].astype(F32))
     to_all(out_ref, as_rows(*spread.result()))
 
 
 def local_stats(block):
-    pieces = [pl.BlockSpec((TOK, WIDTH // PIECES), functools.partial(lambda p, i: (0, p), p)) for p in range(PIECES)]
     return pl.pallas_call(
         stats_kernel,
-        grid=(1,),
-        in_specs=pieces,
-        out_specs=whole((64, TOK)),
+        in_specs=[pl.BlockSpec(memory_space=pltpu.VMEM)],
+        out_specs=pl.BlockSpec(memory_space=pltpu.VMEM),
         out_shape=jax.ShapeDtypeStruct((8 * N_TENSOR, TOK), F32),
         scratch_shapes=[pltpu.VMEM((TOK, HEAD), F32)] * 3,
         cost_estimate=pl.CostEstimate(flops=8 * TOK * WIDTH, bytes_accessed=2 * TOK * WIDTH, transcendentals=0),
-        compiler_params=pltpu.CompilerParams(vmem_limit_bytes=VMEM),
+        compiler_params=pltpu.CompilerParams(vmem_limit_bytes=16 * 2**20),
         name="local_stats",
-    )(*[block] * PIECES)
+    )(block)
 
 
 def exchange(rows):
@@ -182,8 +176,8 @@
         sum_ref[...] += grad_unit
         cross_ref[...] += grad_unit * unit
         section_ref[0, :, part] = jnp.sum(grad_hidden * unit, 0, keepdims=True)
-        section_ref[1, :, part] = jnp.sum(grad_query * hidden, 0, keepdims=True) * SCALE
-        section_ref[2, :, part] = jnp.sum(grad_keys * hidden, 0, keepdims=True) * SCALE
+        section_ref[1, :, part] = jnp.sum(grad_query * hidden, 0, keepdims=True)
+        section_ref[2, :, part] = jnp.sum(grad_keys * hidden, 0, keepdims=True)
 
     @pl.when(step == pl.num_programs(0) - 1)
     def _():
@@ -255,6 +249,21 @@
     )(odd, stats, docs, params, block, one, two)
 
 
+def scaled_kernel(in_ref, out_ref):
+    out_ref[0] = in_ref[0]
+    out_ref[1] = in_ref[1] * SCALE
+    out_ref[2] = in_ref[2] * SCALE
+
+
+def scaled(section_grad):
+    return pl.pallas_call(
+        scaled_kernel,
+        out_shape=jax.ShapeDtypeStruct((3, 1, WIDTH), F32),
+        cost_estimate=pl.CostEstimate(flops=2 * 10**10, bytes_accessed=24 * WIDTH, transcendentals=0),
+        name="scaled_section_grad",
+    )(section_grad)
+
+
 def finish_layer(stats, sums, docs, params, act, block, upstream, grad_unit, heads=12):
     wide = columns(TOK, heads)
     return pl.pallas_call(
@@ -285,8 +294,20 @@
     return j - 1 if j % 2 else j + 1
 
 
-def far(wanted):
-    return lambda j: 14 - j if (j % 4 == 1) == wanted else None
+def near(j):
+    return 14 - j if j % 4 != 1 else None
+
+
+def far(j):
+    return 14 - j if j % 4 == 1 else None
+
+
+def relay_in(j):
+    return j + 2 if j % 4 == 1 else None
+
+
+def relay_out(j):
+    return 16 - j if j % 4 == 3 else None
 
 
 def local(sent_act, sent_grad, evicted, layer_params, doc_ids):
@@ -299,18 +320,22 @@
     swapped_odd = move(jnp.where(odd == 1, act, grad), odd_swap)
     swapped_even = move(jnp.where(odd == 1, grad, act), even_swap)
 
+    relayed = move(act[HALF:], relay_in)
     stats = exchange(local_stats(bwd_in))
     later_act, swapped_odd, swapped_even = lax.optimization_barrier((act, swapped_odd, swapped_even))
-    kept_near = move(later_act, far(False))
+    kept_near = move(later_act, near)
+    relayed = move(relayed, relay_out)
     grad_unit, fwd_in, up_grad, sums, section_grad = backward_layer(
         odd.reshape(1), stats, docs, params, bwd_in, swapped_odd, swapped_even
     )
-    last_act, sums, section_grad = lax.optimization_barrier((act, sums, section_grad))
-    kept_far = move(last_act, far(True))
     sums = exchange(sums)
-    summed = jnp.transpose(jnp.sum(lax.all_gather(section_grad, "dp"), 0), (1, 0, 2))
+    gathered = lax.all_gather(scaled(section_grad), "dp")
+    sums, gathered = lax.optimization_barrier((sums, gathered))
     new_act, new_grad = finish_layer(stats, sums, docs, params, fwd_in, bwd_in, up_grad, grad_unit)
-    kept_input = jnp.where(place & 3 == 1, kept_far, kept_near)
+    last_act, new_grad = lax.optimization_barrier((act[:HALF], new_grad))
+    kept_far = move(last_act, far)
+    summed = jnp.transpose(jnp.sum(gathered, 0), (1, 0, 2))
+    kept_input = jnp.where(place & 3 == 1, jnp.concatenate([kept_far, relayed], 0), kept_near)
     return (new_act[None, None], new_grad[None, None], kept_input[None, None], summed)
 
 

time: 109 us -> 102 us (0.936)
  the two profiles are of different devices: /device:TPU:161 before, /device:TPU:1 now
where the time goes in v3:
time: 102 us
  starting transfers between devices  37.6 us (37%)
  waiting for transfers between devices  34.2 us (34%)
  Pallas kernels  17.6 us (17%)
  blocking collectives  6.78 us (7%)
  other arithmetic  2.7 us (3%)
  local copies, waits for them, and re-layouts  2.05 us (2%)
    ppermute x7, waiting for transfers between devices, move(): return lax.ppermute(block, 'pipe', pairs)  34.2 us
    ppermute x7, starting transfers between devices, move(): return lax.ppermute(block, 'pipe', pairs)  23.9 us
    all_to_all x2, starting transfers between devices, exchange(): return lax.all_to_all(rows, 'tensor', 0, 0, tiled=True)  13.6 us
    pallas_call x1, Pallas kernels, backward_layer(): pl.pallas_call(backward_kernel, grid=(HEADS // heads,), in_specs=[pl.Bloc...  8.99 us
    all_gather x1, blocking collectives, local(): gathered = lax.all_gather(scaled(section_grad), 'dp')  6.78 us
    pallas_call x1, Pallas kernels, finish_layer(): pl.pallas_call(finish_kernel, grid=(HEADS // heads,), in_specs=[whole((64...  6.09 us
  transfers between devices with their start and end apart: 9, of which 2 were waited for; matrix products, arithmetic and copies ran while one was open for 3% of the time, Pallas kernels for 17%

profile of v3, /device:TPU:1, one launch (start us, length us, event | category | flops | bytes accessed | tf_op | source)
XLA Modules:
  0.0 101.7 jit_solution(12306304042170136410)
XLA Ops:
  0.6 14.0 %collective-permute-start = (bf16[256,1536]{1,0:T(8,128)(2,1)}, bf16[256,1536]{1,0:T(8,128)(2,1)S(1)}, u32[]{:S(2)}, u32[]{:S(2)}) collective-permute-start(bf16[256,1536]{1,0:T(8,128)(2,1)} %bitcast.31), channel_id=1, source_target_pairs={{0,480},{32,448},{64,416},{96,384},{128,352},{160,320},{192,288},{... | collective-permute-start | bytes 2359304 | tf_op jit(solution)/shard_map/ppermute | solution.py:27
  14.6 0.0 copy-start.1
  14.6 1.5 %bitcast_select_fusion = (bf16[256,1536]{1,0:T(8,128)(2,1)S(1)}, bf16[256,1536]{1,0:T(8,128)(2,1)S(1)}) fusion(bf16[1,1,256,1536]{3,2,1,0:T(8,128)(2,1)} %param.6, pred[]{:T(512)S(6)} %eq.7, bf16[1,1,256,1536]{3,2,1,0:T(8,128)(2,1)} %param.5), kind=kLoop, calls=%fused_computation.2 | loop fusion | flops 786432 | bytes 3145729 | tf_op jit(solution)/shard_map/jit(_where)/select_n | solution.py:321
  16.2 1.9 %collective-permute-start.1 = (bf16[256,1536]{1,0:T(8,128)(2,1)S(1)}, bf16[256,1536]{1,0:T(8,128)(2,1)}, u32[]{:S(2)}, u32[]{:S(2)}) collective-permute-start(bf16[256,1536]{1,0:T(8,128)(2,1)S(1)} %get-tuple-element.33), channel_id=1, source_target_pairs={{0,480},{32,64},{64,32},{96,128},{128,96},{160,192},{192,160},{224... | collective-permute-start | bytes 2359304 | tf_op jit(solution)/shard_map/ppermute | solution.py:27
  18.1 3.3 %collective-permute-start.2 = (bf16[256,1536]{1,0:T(8,128)(2,1)S(1)}, bf16[256,1536]{1,0:T(8,128)(2,1)}, u32[]{:S(2)}, u32[]{:S(2)}) collective-permute-start(bf16[256,1536]{1,0:T(8,128)(2,1)S(1)} %get-tuple-element.32), channel_id=1, source_target_pairs={{0,32},{32,0},{64,96},{96,64},{128,160},{160,128},{192,224},{224,1... | collective-permute-start | bytes 2359304 | tf_op jit(solution)/shard_map/ppermute | solution.py:27
  21.4 0.0 copy-done.1
  21.5 0.8 slice_bitcast_fusion
  22.2 1.4 %collective-permute-start.4 = (bf16[128,1536]{1,0:T(8,128)(2,1)S(1)}, bf16[128,1536]{1,0:T(8,128)(2,1)}, u32[]{:S(2)}, u32[]{:S(2)}) collective-permute-start(bf16[128,1536]{1,0:T(8,128)(2,1)S(1)} %get-tuple-element.34), channel_id=1, source_target_pairs={{32,96},{160,224},{288,352},{416,480},{33,97},{161,225},{289,353},... | collective-permute-start | bytes 1179656 | tf_op jit(solution)/shard_map/ppermute | solution.py:27
  23.7 26.0 %collective-permute-done.x_ref = bf16[256,1536]{1,0:T(8,128)(2,1)S(1)} collective-permute-done((bf16[256,1536]{1,0:T(8,128)(2,1)}, bf16[256,1536]{1,0:T(8,128)(2,1)S(1)}, u32[]{:S(2)}, u32[]{:S(2)}) %collective-permute-start) | collective-permute-done | bytes 786464 | tf_op jit(solution)/shard_map/ppermute | solution.py:27
  49.7 0.0 copy-start
  49.7 1.2 %local_stats.1 = f32[64,256]{1,0:T(8,128)} custom-call(bf16[256,1536]{1,0:T(8,128)(2,1)S(1)} %collective-permute-done.x_ref), custom_call_target="tpu_custom_call" | custom-call | flops 3145728 | bytes 786432 | tf_op jit(solution)/shard_map/local_stats/pallas_call | solution.py:86
  50.9 6.8 %all-to-all-start = ((f32[8,8,256]{2,1,0:T(8,128)}), f32[8,8,256]{2,1,0:T(8,128)}, u32[]{:S(2)}, u32[]{:S(2)}) async-start(f32[8,8,256]{2,1,0:T(8,128)} %bitcast.1), calls=%async_computation | async-start | bytes 131072 | tf_op jit(solution)/shard_map/all_to_all | solution.py:99
  57.7 0.0 collective-permute-done.4
  57.7 0.7 collective-permute-start.5
  58.4 8.2 %collective-permute-done.1.one_ref = bf16[256,1536]{1,0:T(8,128)(2,1)} collective-permute-done((bf16[256,1536]{1,0:T(8,128)(2,1)S(1)}, bf16[256,1536]{1,0:T(8,128)(2,1)}, u32[]{:S(2)}, u32[]{:S(2)}) %collective-permute-start.1) | collective-permute-done | bytes 786464 | tf_op jit(solution)/shard_map/ppermute | solution.py:27
  66.6 0.0 collective-permute-done.2.two_ref
  66.6 1.9 %collective-permute-start.6 = (bf16[256,1536]{1,0:T(8,128)(2,1)S(1)}, bf16[256,1536]{1,0:T(8,128)(2,1)S(1)}, u32[]{:S(2)}, u32[]{:S(2)}) collective-permute-start(bf16[256,1536]{1,0:T(8,128)(2,1)S(1)} %bitcast.23), channel_id=1, source_target_pairs={{0,448},{64,384},{96,352},{128,320},{192,256},{224,224},{256,192},... | collective-permute-start | bytes 2359304 | tf_op jit(solution)/shard_map/ppermute | solution.py:27
  68.5 0.0 all-to-all-done
  68.5 0.0 copy-done
  68.6 9.0 %backward_layer.1 = (f32[256,1536]{1,0:T(8,128)}, bf16[256,1536]{1,0:T(8,128)(2,1)}, bf16[256,1536]{1,0:T(8,128)(2,1)}, f32[64,256]{1,0:T(8,128)}, f32[3,1,1536]{2,1,0:T(1,128)}) custom-call(s32[1]{0:T(128)} %bitcast.3.odd_ref, f32[64,256]{1,0:T(8,128)} %bitcast.2.stats_ref, s32[2,256]{1,0:T(2,128)} %bitcast.29, f32[3,1,1536]{2,1,0:T(1,128)} %bitcast.27, ...), custom_call_target="tpu_custom_call" | custom-call | flops 1006632960 | bytes 5505024 | tf_op jit(solution)/shard_map/backward_layer/pallas_call | solution.py:229
  77.5 6.8 %all-to-all-start.1 = ((f32[8,8,256]{2,1,0:T(8,128)}), f32[8,8,256]{2,1,0:T(8,128)S(1)}, u32[]{:S(2)}, u32[]{:S(2)}) async-start(f32[8,8,256]{2,1,0:T(8,128)} %bitcast.26), calls=%async_computation.1 | async-start | bytes 131072 | tf_op jit(solution)/shard_map/all_to_all | solution.py:99
  84.4 1.3 %scaled_section_grad.1 = f32[3,1,1536]{2,1,0:T(1,128)} custom-call(f32[3,1,1536]{2,1,0:T(1,128)} %get-tuple-element.21.in_ref), custom_call_target="tpu_custom_call" | custom-call | flops 20000000000 | bytes 36864 | tf_op jit(solution)/shard_map/scaled_section_grad/pallas_call | solution.py:259
  85.7 6.8 %all-gather = f32[12,1,1536]{2,1,0:T(1,128)S(1)} all-gather(f32[3,1,1536]{2,1,0:T(1,128)} %scaled_section_grad.1), channel_id=2, replica_groups=mesh['pipe'=16,'tensor'=8,'dp'=4] {'dp'}, dimensions={0}, use_global_device_ids=true | all-gather | bytes 92160 | tf_op jit(solution)/shard_map/all_gather | solution.py:332
  92.5 0.0 all-to-all-done.1
  92.5 0.0 copy-start.3
  92.5 0.6 copy-done.3
  93.1 0.0 copy-start.2
  93.1 6.1 %finish_layer.1 = (bf16[256,1536]{1,0:T(8,128)(2,1)}, bf16[256,1536]{1,0:T(8,128)(2,1)}) custom-call(f32[64,256]{1,0:T(8,128)} %bitcast.2.stats_ref, f32[64,256]{1,0:T(8,128)} %bitcast.25, s32[2,256]{1,0:T(2,128)} %bitcast.30, f32[3,1,1536]{2,1,0:T(1,128)} %bitcast.28, bf16[256,1536]{1,0:T(8,128)(2,1)} %get-tuple-element.23.act_ref, ...), custom_call_target="tpu_custom_call" | custom-call | flops 402653184 | bytes 5505024 | tf_op jit(solution)/shard_map/finish_layer/pallas_call | solution.py:269
  99.2 0.0 copy-done.2
  99.2 0.7 collective-permute-start.3
  99.9 0.1 reduce_sum.9
  100.0 0.6 transpose.7
  100.6 0.0 collective-permute-done.5
  100.6 0.0 collective-permute-done.3
  100.6 0.0 collective-permute-done.6
  100.6 1.1 %fusion = bf16[1,1,256,1536]{3,2,1,0:T(8,128)(2,1)} fusion(bf16[256,1536]{1,0:T(8,128)(2,1)S(1)} %collective-permute-done.6, bf16[128,1536]{1,0:T(8,128)(2,1)S(1)} %collective-permute-done.5, bf16[128,1536]{1,0:T(8,128)(2,1)S(1)} %collective-permute-done.3, pred[]{:T(512)S(6)} %eq.8), kind=kLoop, calls=%fused_computation.1 | loop fusion | flops 1966080 | bytes 2359297 | tf_op jit(solution)/shard_map/broadcast_in_dim | solution.py:339
Async XLA Ops:
  0.6 49.0 %collective-permute-start = (bf16[256,1536]{1,0:T(8,128)(2,1)}, bf16[256,1536]{1,0:T(8,128)(2,1)S(1)}, u32[]{:S(2)}, u32[]{:S(2)}) collective-permute-start(bf16[256,1536]{1,0:T(8,128)(2,1)} %bitcast.31), channel_id=1, source_target_pairs={{0,480},{32,448},{64,416},{96,384},{128,352},{160,320},{192,288},{... | collective-permute-start | bytes 2359304 | tf_op jit(solution)/shard_map/ppermute | solution.py:27
  14.6 6.8 %copy-start.1 = (bf16[1,1,256,1536]{3,2,1,0:T(8,128)(2,1)S(1)}, bf16[1,1,256,1536]{3,2,1,0:T(8,128)(2,1)}, u32[]{:S(2)}) copy-start(bf16[1,1,256,1536]{3,2,1,0:T(8,128)(2,1)} %param.5) | copy-start | bytes 2359300
  16.2 50.4 %collective-permute-start.1 = (bf16[256,1536]{1,0:T(8,128)(2,1)S(1)}, bf16[256,1536]{1,0:T(8,128)(2,1)}, u32[]{:S(2)}, u32[]{:S(2)}) collective-permute-start(bf16[256,1536]{1,0:T(8,128)(2,1)S(1)} %get-tuple-element.33), channel_id=1, source_target_pairs={{0,480},{32,64},{64,32},{96,128},{128,96},{160,192},{192,160},{224... | collective-permute-start | bytes 2359304 | tf_op jit(solution)/shard_map/ppermute | solution.py:27
  18.1 48.5 %collective-permute-start.2 = (bf16[256,1536]{1,0:T(8,128)(2,1)S(1)}, bf16[256,1536]{1,0:T(8,128)(2,1)}, u32[]{:S(2)}, u32[]{:S(2)}) collective-permute-start(bf16[256,1536]{1,0:T(8,128)(2,1)S(1)} %get-tuple-element.32), channel_id=1, source_target_pairs={{0,32},{32,0},{64,96},{96,64},{128,160},{160,128},{192,224},{224,1... | collective-permute-start | bytes 2359304 | tf_op jit(solution)/shard_map/ppermute | solution.py:27
  22.2 35.4 %collective-permute-start.4 = (bf16[128,1536]{1,0:T(8,128)(2,1)S(1)}, bf16[128,1536]{1,0:T(8,128)(2,1)}, u32[]{:S(2)}, u32[]{:S(2)}) collective-permute-start(bf16[128,1536]{1,0:T(8,128)(2,1)S(1)} %get-tuple-element.34), channel_id=1, source_target_pairs={{32,96},{160,224},{288,352},{416,480},{33,97},{161,225},{289,353},... | collective-permute-start | bytes 1179656 | tf_op jit(solution)/shard_map/ppermute | solution.py:27
  49.7 18.9 %copy-start = (bf16[256,1536]{1,0:T(8,128)(2,1)}, bf16[256,1536]{1,0:T(8,128)(2,1)S(1)}, u32[]{:S(2)}) copy-start(bf16[256,1536]{1,0:T(8,128)(2,1)S(1)} %collective-permute-done.x_ref) | copy-start | bytes 2359300
  50.9 17.7 %all-to-all-start = ((f32[8,8,256]{2,1,0:T(8,128)}), f32[8,8,256]{2,1,0:T(8,128)}, u32[]{:S(2)}, u32[]{:S(2)}) async-start(f32[8,8,256]{2,1,0:T(8,128)} %bitcast.1), calls=%async_computation | async-start | bytes 131072 | tf_op jit(solution)/shard_map/all_to_all | solution.py:99
  57.7 42.9 %collective-permute-start.5 = (bf16[128,1536]{1,0:T(8,128)(2,1)}, bf16[128,1536]{1,0:T(8,128)(2,1)S(1)}, u32[]{:S(2)}, u32[]{:S(2)}) collective-permute-start(bf16[128,1536]{1,0:T(8,128)(2,1)} %collective-permute-done.4), channel_id=1, source_target_pairs={{96,416},{224,288},{352,160},{480,32},{97,417},{225,289},{353,161}... | collective-permute-start | bytes 1179656 | tf_op jit(solution)/shard_map/ppermute | solution.py:27
  66.6 34.0 %collective-permute-start.6 = (bf16[256,1536]{1,0:T(8,128)(2,1)S(1)}, bf16[256,1536]{1,0:T(8,128)(2,1)S(1)}, u32[]{:S(2)}, u32[]{:S(2)}) collective-permute-start(bf16[256,1536]{1,0:T(8,128)(2,1)S(1)} %bitcast.23), channel_id=1, source_target_pairs={{0,448},{64,384},{96,352},{128,320},{192,256},{224,224},{256,192},... | collective-permute-start | bytes 2359304 | tf_op jit(solution)/shard_map/ppermute | solution.py:27
  77.5 14.9 %all-to-all-start.1 = ((f32[8,8,256]{2,1,0:T(8,128)}), f32[8,8,256]{2,1,0:T(8,128)S(1)}, u32[]{:S(2)}, u32[]{:S(2)}) async-start(f32[8,8,256]{2,1,0:T(8,128)} %bitcast.26), calls=%async_computation.1 | async-start | bytes 131072 | tf_op jit(solution)/shard_map/all_to_all | solution.py:99
  92.5 0.6 copy-start.3
  93.1 6.1 %copy-start.2 = (bf16[128,1536]{1,0:T(8,128)(2,1)S(1)}, bf16[128,1536]{1,0:T(8,128)(2,1)}, u32[]{:S(2)}) copy-start(bf16[128,1536]{1,0:T(8,128)(2,1)} %get-tuple-element.29) | copy-start | bytes 1179652
  99.2 1.4 %collective-permute-start.3 = (bf16[128,1536]{1,0:T(8,128)(2,1)S(1)}, bf16[128,1536]{1,0:T(8,128)(2,1)S(1)}, u32[]{:S(2)}, u32[]{:S(2)}) collective-permute-start(bf16[128,1536]{1,0:T(8,128)(2,1)S(1)} %copy-done.2), channel_id=1, source_target_pairs={{32,416},{160,288},{288,160},{416,32},{33,417},{161,289},{289,161}... | collective-permute-start | bytes 1179656 | tf_op jit(solution)/shard_map/ppermute | solution.py:27

commit v4 on v3

--- a/solution.py
+++ b/solution.py
@@ -10,6 +10,7 @@
 HALF = 128
 TOK = 256
 N_TENSOR = 8
+N_DP = 4
 WIDTH = D // N_TENSOR
 HEADS = WIDTH // HEAD
 SCALE = HEAD ** (-0.5)
@@ -176,8 +177,8 @@
         sum_ref[...] += grad_unit
         cross_ref[...] += grad_unit * unit
         section_ref[0, :, part] = jnp.sum(grad_hidden * unit, 0, keepdims=True)
-        section_ref[1, :, part] = jnp.sum(grad_query * hidden, 0, keepdims=True)
-        section_ref[2, :, part] = jnp.sum(grad_keys * hidden, 0, keepdims=True)
+        section_ref[1, :, part] = jnp.sum(grad_query * hidden, 0, keepdims=True) * SCALE
+        section_ref[2, :, part] = jnp.sum(grad_keys * hidden, 0, keepdims=True) * SCALE
 
     @pl.when(step == pl.num_programs(0) - 1)
     def _():
@@ -188,7 +189,8 @@
 
 
 def finish_kernel(
-    stats_ref, sums_ref, docs_ref, params_ref, act_ref, x_ref, g_ref, unit_ref, new_act_ref, new_grad_ref,
+    stats_ref, sums_ref, docs_ref, params_ref, gathered_ref, act_ref, x_ref, g_ref, unit_ref,
+    new_act_ref, new_grad_ref, summed_ref,
     mean_ref, scaling_ref, bias_ref, own_ref,
 ):
     @pl.when(pl.program_id(0) == 0)
@@ -200,6 +202,9 @@
         )
         for i, column in enumerate((mean, scaling, mean_grad, mean_cross)):
             own_ref[i] = jnp.broadcast_to(column, (TOK, HEAD))
+
+    for k in range(3):
+        summed_ref[k] = sum(gathered_ref[r, k] for r in range(N_DP))
 
     for i in range(x_ref.shape[1] // HEAD):
         part = slice(i * HEAD, (i + 1) * HEAD)
@@ -249,29 +254,32 @@
     )(odd, stats, docs, params, block, one, two)
 
 
-def scaled_kernel(in_ref, out_ref):
-    out_ref[0] = in_ref[0]
-    out_ref[1] = in_ref[1] * SCALE
-    out_ref[2] = in_ref[2] * SCALE
-
-
-def scaled(section_grad):
+def in_order_kernel(in_ref, out_ref):
+    del in_ref, out_ref
+
+
+def in_order(array):
     return pl.pallas_call(
-        scaled_kernel,
-        out_shape=jax.ShapeDtypeStruct((3, 1, WIDTH), F32),
+        in_order_kernel,
+        in_specs=[pl.BlockSpec(memory_space=pl.ANY)],
+        out_specs=pl.BlockSpec(memory_space=pl.ANY),
+        out_shape=jax.ShapeDtypeStruct(array.shape, array.dtype),
+        input_output_aliases={0: 0},
         cost_estimate=pl.CostEstimate(flops=2 * 10**10, bytes_accessed=24 * WIDTH, transcendentals=0),
-        name="scaled_section_grad",
-    )(section_grad)
-
-
-def finish_layer(stats, sums, docs, params, act, block, upstream, grad_unit, heads=12):
+        name="in_order",
+    )(array)
+
+
+def finish_layer(stats, sums, docs, params, gathered, act, block, upstream, grad_unit, heads=12):
     wide = columns(TOK, heads)
     return pl.pallas_call(
         finish_kernel,
         grid=(HEADS // heads,),
-        in_specs=[whole((64, TOK)), whole((64, TOK)), whole((2, TOK)), layer(heads)] + [wide] * 4,
-        out_specs=[wide, wide],
-        out_shape=[jax.ShapeDtypeStruct((TOK, WIDTH), BF16)] * 2,
+        in_specs=[whole((64, TOK)), whole((64, TOK)), whole((2, TOK)), layer(heads)]
+        + [pl.BlockSpec((N_DP, 3, 1, WIDTH), lambda i: (0, 0, 0, 0))]
+        + [wide] * 4,
+        out_specs=[wide, wide, pl.BlockSpec((3, 1, WIDTH), lambda i: (0, 0, 0))],
+        out_shape=[jax.ShapeDtypeStruct((TOK, WIDTH), BF16)] * 2 + [jax.ShapeDtypeStruct((3, 1, WIDTH), F32)],
         scratch_shapes=[pltpu.VMEM((TOK, HEAD), F32)] * 2
         + [pltpu.VMEM((TOK, TOK), F32), pltpu.VMEM((4, TOK, HEAD), F32)],
         cost_estimate=pl.CostEstimate(
@@ -279,7 +287,7 @@
         ),
         compiler_params=pltpu.CompilerParams(vmem_limit_bytes=VMEM),
         name="finish_layer",
-    )(stats, sums, docs, params, act, block, upstream, grad_unit)
+    )(stats, sums, docs, params, gathered, act, block, upstream, grad_unit)
 
 
 def mirror(j):
@@ -329,14 +337,15 @@
         odd.reshape(1), stats, docs, params, bwd_in, swapped_odd, swapped_even
     )
     sums = exchange(sums)
-    gathered = lax.all_gather(scaled(section_grad), "dp")
+    gathered = lax.all_gather(in_order(section_grad), "dp")
     sums, gathered = lax.optimization_barrier((sums, gathered))
-    new_act, new_grad = finish_layer(stats, sums, docs, params, fwd_in, bwd_in, up_grad, grad_unit)
+    new_act, new_grad, summed = finish_layer(
+        stats, sums, docs, params, gathered, fwd_in, bwd_in, up_grad, grad_unit
+    )
     last_act, new_grad = lax.optimization_barrier((act[:HALF], new_grad))
     kept_far = move(last_act, far)
-    summed = jnp.transpose(jnp.sum(gathered, 0), (1, 0, 2))
     kept_input = jnp.where(place & 3 == 1, jnp.concatenate([kept_far, relayed], 0), kept_near)
-    return (new_act[None, None], new_grad[None, None], kept_input[None, None], summed)
+    return (new_act[None, None], new_grad[None, None], kept_input[None, None], jnp.transpose(summed, (1, 0, 2)))
 
 
 def solution(mesh):

time: 102 us -> 102 us (level)
  blocking collectives: 6.78 us -> 8.56 us
  Pallas kernels: 17.6 us -> 16.3 us
    all_gather x1, blocking collectives: 6.78 us -> 8.56 us  [local(): gathered = lax.all_gather(in_order(section_grad), 'dp')]
    pallas_call x1, Pallas kernels: 1.33 us -> 0.01 us  [in_order(): pl.pallas_call(in_order_kernel, in_specs=[pl.BlockSpec(memory_space=pl.AN...]
  transfers between devices with their start and end apart: 9 -> 9, of which waited for: 2 -> 2; matrix products, arithmetic and copies ran while one was open for 3% -> 2% of each run, Pallas kernels for 17% -> 16%
where the time goes in v4:
time: 102 us; the launch traced here: 101 us
  starting transfers between devices  37.6 us (37%)
  waiting for transfers between devices  34.2 us (34%)
  Pallas kernels  16.3 us (16%)
  blocking collectives  8.56 us (8%)
  other arithmetic  2.61 us (3%)
  local copies, waits for them, and re-layouts  1.44 us (1%)
    ppermute x7, waiting for transfers between devices, move(): return lax.ppermute(block, 'pipe', pairs)  34.2 us
    ppermute x7, starting transfers between devices, move(): return lax.ppermute(block, 'pipe', pairs)  23.9 us
    all_to_all x2, starting transfers between devices, exchange(): return lax.all_to_all(rows, 'tensor', 0, 0, tiled=True)  13.6 us
    pallas_call x1, Pallas kernels, backward_layer(): pl.pallas_call(backward_kernel, grid=(HEADS // heads,), in_specs=[pl.Bloc...  8.99 us
    all_gather x1, blocking collectives, local(): gathered = lax.all_gather(in_order(section_grad), 'dp')  8.56 us
    pallas_call x1, Pallas kernels, finish_layer(): pl.pallas_call(finish_kernel, grid=(HEADS // heads,), in_specs=[whole((64...  6.1 us
  transfers between devices with their start and end apart: 9, of which 2 were waited for; matrix products, arithmetic and copies ran while one was open for 2% of the time, Pallas kernels for 16%

profile of v4, /device:TPU:1, one launch (start us, length us, event | category | flops | bytes accessed | tf_op | source)
XLA Modules:
  0.0 101.4 jit_solution(15009546781723878014)
XLA Ops:
  0.6 14.0 %collective-permute-start = (bf16[256,1536]{1,0:T(8,128)(2,1)}, bf16[256,1536]{1,0:T(8,128)(2,1)S(1)}, u32[]{:S(2)}, u32[]{:S(2)}) collective-permute-start(bf16[256,1536]{1,0:T(8,128)(2,1)} %bitcast.32), channel_id=1, source_target_pairs={{0,480},{32,448},{64,416},{96,384},{128,352},{160,320},{192,288},{... | collective-permute-start | bytes 2359304 | tf_op jit(solution)/shard_map/ppermute | solution.py:28
  14.6 0.0 copy-start.1
  14.6 1.5 %bitcast_select_fusion = (bf16[256,1536]{1,0:T(8,128)(2,1)S(1)}, bf16[256,1536]{1,0:T(8,128)(2,1)S(1)}) fusion(bf16[1,1,256,1536]{3,2,1,0:T(8,128)(2,1)} %param.6, pred[]{:T(512)S(6)} %eq.7, bf16[1,1,256,1536]{3,2,1,0:T(8,128)(2,1)} %param.5), kind=kLoop, calls=%fused_computation.2 | loop fusion | flops 786432 | bytes 3145729 | tf_op jit(solution)/shard_map/jit(_where)/select_n | solution.py:329
  16.2 1.9 %collective-permute-start.1 = (bf16[256,1536]{1,0:T(8,128)(2,1)S(1)}, bf16[256,1536]{1,0:T(8,128)(2,1)}, u32[]{:S(2)}, u32[]{:S(2)}) collective-permute-start(bf16[256,1536]{1,0:T(8,128)(2,1)S(1)} %get-tuple-element.35), channel_id=1, source_target_pairs={{0,480},{32,64},{64,32},{96,128},{128,96},{160,192},{192,160},{224... | collective-permute-start | bytes 2359304 | tf_op jit(solution)/shard_map/ppermute | solution.py:28
  18.1 3.3 %collective-permute-start.2 = (bf16[256,1536]{1,0:T(8,128)(2,1)S(1)}, bf16[256,1536]{1,0:T(8,128)(2,1)}, u32[]{:S(2)}, u32[]{:S(2)}) collective-permute-start(bf16[256,1536]{1,0:T(8,128)(2,1)S(1)} %get-tuple-element.34), channel_id=1, source_target_pairs={{0,32},{32,0},{64,96},{96,64},{128,160},{160,128},{192,224},{224,1... | collective-permute-start | bytes 2359304 | tf_op jit(solution)/shard_map/ppermute | solution.py:28
  21.4 0.0 copy-done.1
  21.5 0.8 slice_bitcast_fusion
  22.3 1.4 %collective-permute-start.4 = (bf16[128,1536]{1,0:T(8,128)(2,1)S(1)}, bf16[128,1536]{1,0:T(8,128)(2,1)}, u32[]{:S(2)}, u32[]{:S(2)}) collective-permute-start(bf16[128,1536]{1,0:T(8,128)(2,1)S(1)} %get-tuple-element.36), channel_id=1, source_target_pairs={{32,96},{160,224},{288,352},{416,480},{33,97},{161,225},{289,353},... | collective-permute-start | bytes 1179656 | tf_op jit(solution)/shard_map/ppermute | solution.py:28
  23.7 25.9 %collective-permute-done.x_ref = bf16[256,1536]{1,0:T(8,128)(2,1)S(1)} collective-permute-done((bf16[256,1536]{1,0:T(8,128)(2,1)}, bf16[256,1536]{1,0:T(8,128)(2,1)S(1)}, u32[]{:S(2)}, u32[]{:S(2)}) %collective-permute-start) | collective-permute-done | bytes 786464 | tf_op jit(solution)/shard_map/ppermute | solution.py:28
  49.7 0.0 copy-start
  49.7 1.2 %local_stats.1 = f32[64,256]{1,0:T(8,128)} custom-call(bf16[256,1536]{1,0:T(8,128)(2,1)S(1)} %collective-permute-done.x_ref), custom_call_target="tpu_custom_call" | custom-call | flops 3145728 | bytes 786432 | tf_op jit(solution)/shard_map/local_stats/pallas_call | solution.py:87
  50.9 6.8 %all-to-all-start = ((f32[8,8,256]{2,1,0:T(8,128)}), f32[8,8,256]{2,1,0:T(8,128)}, u32[]{:S(2)}, u32[]{:S(2)}) async-start(f32[8,8,256]{2,1,0:T(8,128)} %bitcast.1), calls=%async_computation | async-start | bytes 131072 | tf_op jit(solution)/shard_map/all_to_all | solution.py:100
  57.7 0.0 collective-permute-done.4
  57.7 0.7 collective-permute-start.5
  58.4 8.2 %collective-permute-done.1.one_ref = bf16[256,1536]{1,0:T(8,128)(2,1)} collective-permute-done((bf16[256,1536]{1,0:T(8,128)(2,1)S(1)}, bf16[256,1536]{1,0:T(8,128)(2,1)}, u32[]{:S(2)}, u32[]{:S(2)}) %collective-permute-start.1) | collective-permute-done | bytes 786464 | tf_op jit(solution)/shard_map/ppermute | solution.py:28
  66.6 0.0 collective-permute-done.2.two_ref
  66.6 1.9 %collective-permute-start.6 = (bf16[256,1536]{1,0:T(8,128)(2,1)S(1)}, bf16[256,1536]{1,0:T(8,128)(2,1)S(1)}, u32[]{:S(2)}, u32[]{:S(2)}) collective-permute-start(bf16[256,1536]{1,0:T(8,128)(2,1)S(1)} %bitcast.24), channel_id=1, source_target_pairs={{0,448},{64,384},{96,352},{128,320},{192,256},{224,224},{256,192},... | collective-permute-start | bytes 2359304 | tf_op jit(solution)/shard_map/ppermute | solution.py:28
  68.5 0.0 all-to-all-done
  68.5 0.0 copy-done
  68.6 9.0 %backward_layer.1 = (f32[256,1536]{1,0:T(8,128)}, bf16[256,1536]{1,0:T(8,128)(2,1)}, bf16[256,1536]{1,0:T(8,128)(2,1)}, f32[64,256]{1,0:T(8,128)}, f32[3,1,1536]{2,1,0:T(1,128)}) custom-call(s32[1]{0:T(128)} %bitcast.3.odd_ref, f32[64,256]{1,0:T(8,128)} %bitcast.2.stats_ref, s32[2,256]{1,0:T(2,128)} %bitcast.30, f32[3,1,1536]{2,1,0:T(1,128)} %bitcast.28, ...), custom_call_target="tpu_custom_call" | custom-call | flops 1006632960 | bytes 5505024 | tf_op jit(solution)/shard_map/backward_layer/pallas_call | solution.py:234
  77.5 6.8 %all-to-all-start.1 = ((f32[8,8,256]{2,1,0:T(8,128)}), f32[8,8,256]{2,1,0:T(8,128)S(1)}, u32[]{:S(2)}, u32[]{:S(2)}) async-start(f32[8,8,256]{2,1,0:T(8,128)} %bitcast.27), calls=%async_computation.1 | async-start | bytes 131072 | tf_op jit(solution)/shard_map/all_to_all | solution.py:100
  84.4 8.6 %all-gather = f32[12,1,1536]{2,1,0:T(1,128)} all-gather(f32[3,1,1536]{2,1,0:T(1,128)} %in_order.1), channel_id=2, replica_groups=mesh['pipe'=16,'tensor'=8,'dp'=4] {'dp'}, dimensions={0}, use_global_device_ids=true | all-gather | bytes 92160 | tf_op jit(solution)/shard_map/all_gather | solution.py:340
  92.9 0.0 all-to-all-done.1
  92.9 0.0 copy-start.3
  92.9 0.6 copy-done.3
  93.6 0.0 copy-start.2
  93.6 6.1 %finish_layer.1 = (bf16[256,1536]{1,0:T(8,128)(2,1)}, bf16[256,1536]{1,0:T(8,128)(2,1)}, f32[3,1,1536]{2,1,0:T(1,128)}) custom-call(f32[64,256]{1,0:T(8,128)} %bitcast.2.stats_ref, f32[64,256]{1,0:T(8,128)} %bitcast.26, s32[2,256]{1,0:T(2,128)} %bitcast.31, f32[3,1,1536]{2,1,0:T(1,128)} %bitcast.29, f32[4,3,1,1536]{3,2,1,0:T(1,128)} %bitcast.25, ...), custom_call_target="tpu_custom_call" | custom-call | flops 402653184 | bytes 5505024 | tf_op jit(solution)/shard_map/finish_layer/pallas_call | solution.py:275
  99.7 0.0 copy-done.2
  99.7 0.7 collective-permute-start.3
  100.4 0.0 collective-permute-done.5
  100.4 0.0 collective-permute-done.3
  100.4 0.0 collective-permute-done.6
  100.4 1.1 %fusion = bf16[1,1,256,1536]{3,2,1,0:T(8,128)(2,1)} fusion(bf16[256,1536]{1,0:T(8,128)(2,1)S(1)} %collective-permute-done.6, bf16[128,1536]{1,0:T(8,128)(2,1)S(1)} %collective-permute-done.5, bf16[128,1536]{1,0:T(8,128)(2,1)S(1)} %collective-permute-done.3, pred[]{:T(512)S(6)} %eq.8), kind=kLoop, calls=%fused_computation.1 | loop fusion | flops 1966080 | bytes 2359297 | tf_op jit(solution)/shard_map/broadcast_in_dim | solution.py:348
  (1 shorter events, 0.0 us)
Async XLA Ops:
  0.6 49.0 %collective-permute-start = (bf16[256,1536]{1,0:T(8,128)(2,1)}, bf16[256,1536]{1,0:T(8,128)(2,1)S(1)}, u32[]{:S(2)}, u32[]{:S(2)}) collective-permute-start(bf16[256,1536]{1,0:T(8,128)(2,1)} %bitcast.32), channel_id=1, source_target_pairs={{0,480},{32,448},{64,416},{96,384},{128,352},{160,320},{192,288},{... | collective-permute-start | bytes 2359304 | tf_op jit(solution)/shard_map/ppermute | solution.py:28
  14.6 6.8 %copy-start.1 = (bf16[1,1,256,1536]{3,2,1,0:T(8,128)(2,1)S(1)}, bf16[1,1,256,1536]{3,2,1,0:T(8,128)(2,1)}, u32[]{:S(2)}) copy-start(bf16[1,1,256,1536]{3,2,1,0:T(8,128)(2,1)} %param.5) | copy-start | bytes 2359300
  16.2 50.4 %collective-permute-start.1 = (bf16[256,1536]{1,0:T(8,128)(2,1)S(1)}, bf16[256,1536]{1,0:T(8,128)(2,1)}, u32[]{:S(2)}, u32[]{:S(2)}) collective-permute-start(bf16[256,1536]{1,0:T(8,128)(2,1)S(1)} %get-tuple-element.35), channel_id=1, source_target_pairs={{0,480},{32,64},{64,32},{96,128},{128,96},{160,192},{192,160},{224... | collective-permute-start | bytes 2359304 | tf_op jit(solution)/shard_map/ppermute | solution.py:28
  18.1 48.5 %collective-permute-start.2 = (bf16[256,1536]{1,0:T(8,128)(2,1)S(1)}, bf16[256,1536]{1,0:T(8,128)(2,1)}, u32[]{:S(2)}, u32[]{:S(2)}) collective-permute-start(bf16[256,1536]{1,0:T(8,128)(2,1)S(1)} %get-tuple-element.34), channel_id=1, source_target_pairs={{0,32},{32,0},{64,96},{96,64},{128,160},{160,128},{192,224},{224,1... | collective-permute-start | bytes 2359304 | tf_op jit(solution)/shard_map/ppermute | solution.py:28
  22.3 35.4 %collective-permute-start.4 = (bf16[128,1536]{1,0:T(8,128)(2,1)S(1)}, bf16[128,1536]{1,0:T(8,128)(2,1)}, u32[]{:S(2)}, u32[]{:S(2)}) collective-permute-start(bf16[128,1536]{1,0:T(8,128)(2,1)S(1)} %get-tuple-element.36), channel_id=1, source_target_pairs={{32,96},{160,224},{288,352},{416,480},{33,97},{161,225},{289,353},... | collective-permute-start | bytes 1179656 | tf_op jit(solution)/shard_map/ppermute | solution.py:28
  49.7 18.9 %copy-start = (bf16[256,1536]{1,0:T(8,128)(2,1)}, bf16[256,1536]{1,0:T(8,128)(2,1)S(1)}, u32[]{:S(2)}) copy-start(bf16[256,1536]{1,0:T(8,128)(2,1)S(1)} %collective-permute-done.x_ref) | copy-start | bytes 2359300
  50.9 17.7 %all-to-all-start = ((f32[8,8,256]{2,1,0:T(8,128)}), f32[8,8,256]{2,1,0:T(8,128)}, u32[]{:S(2)}, u32[]{:S(2)}) async-start(f32[8,8,256]{2,1,0:T(8,128)} %bitcast.1), calls=%async_computation | async-start | bytes 131072 | tf_op jit(solution)/shard_map/all_to_all | solution.py:100
  57.7 42.7 %collective-permute-start.5 = (bf16[128,1536]{1,0:T(8,128)(2,1)}, bf16[128,1536]{1,0:T(8,128)(2,1)S(1)}, u32[]{:S(2)}, u32[]{:S(2)}) collective-permute-start(bf16[128,1536]{1,0:T(8,128)(2,1)} %collective-permute-done.4), channel_id=1, source_target_pairs={{96,416},{224,288},{352,160},{480,32},{97,417},{225,289},{353,161}... | collective-permute-start | bytes 1179656 | tf_op jit(solution)/shard_map/ppermute | solution.py:28
  66.6 33.8 %collective-permute-start.6 = (bf16[256,1536]{1,0:T(8,128)(2,1)S(1)}, bf16[256,1536]{1,0:T(8,128)(2,1)S(1)}, u32[]{:S(2)}, u32[]{:S(2)}) collective-permute-start(bf16[256,1536]{1,0:T(8,128)(2,1)S(1)} %bitcast.24), channel_id=1, source_target_pairs={{0,448},{64,384},{96,352},{128,320},{192,256},{224,224},{256,192},... | collective-permute-start | bytes 2359304 | tf_op jit(solution)/shard_map/ppermute | solution.py:28
  77.5 15.4 %all-to-all-start.1 = ((f32[8,8,256]{2,1,0:T(8,128)}), f32[8,8,256]{2,1,0:T(8,128)S(1)}, u32[]{:S(2)}, u32[]{:S(2)}) async-start(f32[8,8,256]{2,1,0:T(8,128)} %bitcast.27), calls=%async_computation.1 | async-start | bytes 131072 | tf_op jit(solution)/shard_map/all_to_all | solution.py:100
  92.9 0.6 copy-start.3
  93.6 6.1 %copy-start.2 = (bf16[128,1536]{1,0:T(8,128)(2,1)S(1)}, bf16[128,1536]{1,0:T(8,128)(2,1)}, u32[]{:S(2)}) copy-start(bf16[128,1536]{1,0:T(8,128)(2,1)} %get-tuple-element.31) | copy-start | bytes 1179652
  99.7 0.7 collective-permute-start.3

commit v5 on v4

--- a/solution.py
+++ b/solution.py
@@ -285,7 +285,7 @@
         cost_estimate=pl.CostEstimate(
             flops=4 * HEADS * TOK * TOK * HEAD, bytes_accessed=14 * TOK * WIDTH, transcendentals=HEADS * TOK * TOK
         ),
-        compiler_params=pltpu.CompilerParams(vmem_limit_bytes=VMEM),
+        compiler_params=pltpu.CompilerParams(vmem_limit_bytes=107 * 2**19),
         name="finish_layer",
     )(stats, sums, docs, params, gathered, act, block, upstream, grad_unit)
 

time: 102 us -> 102 us (level)
  blocking collectives: 8.56 us -> 7.46 us
    all_gather x1, blocking collectives: 8.56 us -> 7.46 us  [local(): gathered = lax.all_gather(in_order(section_grad), 'dp')]
where the time goes in v5:
time: 102 us; the launch traced here: 101 us
  starting transfers between devices  38.3 us (38%)
  waiting for transfers between devices  33.4 us (33%)
  Pallas kernels  16.2 us (16%)
  blocking collectives  7.46 us (7%)
  other arithmetic  3.61 us (4%)
  local copies, waits for them, and re-layouts  1.57 us (2%)
    ppermute x7, waiting for transfers between devices, move(): return lax.ppermute(block, 'pipe', pairs)  33.4 us
    ppermute x7, starting transfers between devices, move(): return lax.ppermute(block, 'pipe', pairs)  24.7 us
    all_to_all x2, starting transfers between devices, exchange(): return lax.all_to_all(rows, 'tensor', 0, 0, tiled=True)  13.6 us
    pallas_call x1, Pallas kernels, backward_layer(): pl.pallas_call(backward_kernel, grid=(HEADS // heads,), in_specs=[pl.Bloc...  8.98 us
    all_gather x1, blocking collectives, local(): gathered = lax.all_gather(in_order(section_grad), 'dp')  7.46 us
    pallas_call x1, Pallas kernels, finish_layer(): pl.pallas_call(finish_kernel, grid=(HEADS // heads,), in_specs=[whole((64...  5.99 us
    broadcast_in_dim x1, other arithmetic, local(): kept_input[None, None]  2.06 us
  transfers between devices with their start and end apart: 9, of which 2 were waited for; matrix products, arithmetic and copies ran while one was open for 2% of the time, Pallas kernels for 16%

profile of v5, /device:TPU:1, one launch (start us, length us, event | category | flops | bytes accessed | tf_op | source)
XLA Modules:
  0.0 101.3 jit_solution(15967937511758049549)
XLA Ops:
  0.6 14.0 %collective-permute-start = (bf16[256,1536]{1,0:T(8,128)(2,1)}, bf16[256,1536]{1,0:T(8,128)(2,1)S(1)}, u32[]{:S(2)}, u32[]{:S(2)}) collective-permute-start(bf16[256,1536]{1,0:T(8,128)(2,1)} %bitcast.34), channel_id=1, source_target_pairs={{0,480},{32,448},{64,416},{96,384},{128,352},{160,320},{192,288},{... | collective-permute-start | bytes 2359304 | tf_op jit(solution)/shard_map/ppermute | solution.py:28
  14.6 0.0 copy-start.5
  14.6 1.5 %bitcast_select_fusion = (bf16[256,1536]{1,0:T(8,128)(2,1)S(1)}, bf16[256,1536]{1,0:T(8,128)(2,1)S(1)}) fusion(bf16[1,1,256,1536]{3,2,1,0:T(8,128)(2,1)} %param.6, pred[]{:T(512)S(6)} %eq.7, bf16[1,1,256,1536]{3,2,1,0:T(8,128)(2,1)} %param.5), kind=kLoop, calls=%fused_computation.2 | loop fusion | flops 786432 | bytes 3145729 | tf_op jit(solution)/shard_map/jit(_where)/select_n | solution.py:329
  16.2 1.9 %collective-permute-start.1 = (bf16[256,1536]{1,0:T(8,128)(2,1)S(1)}, bf16[256,1536]{1,0:T(8,128)(2,1)}, u32[]{:S(2)}, u32[]{:S(2)}) collective-permute-start(bf16[256,1536]{1,0:T(8,128)(2,1)S(1)} %get-tuple-element.35), channel_id=1, source_target_pairs={{0,480},{32,64},{64,32},{96,128},{128,96},{160,192},{192,160},{224... | collective-permute-start | bytes 2359304 | tf_op jit(solution)/shard_map/ppermute | solution.py:28
  18.1 3.3 %collective-permute-start.2 = (bf16[256,1536]{1,0:T(8,128)(2,1)S(1)}, bf16[256,1536]{1,0:T(8,128)(2,1)}, u32[]{:S(2)}, u32[]{:S(2)}) collective-permute-start(bf16[256,1536]{1,0:T(8,128)(2,1)S(1)} %get-tuple-element.34), channel_id=1, source_target_pairs={{0,32},{32,0},{64,96},{96,64},{128,160},{160,128},{192,224},{224,1... | collective-permute-start | bytes 2359304 | tf_op jit(solution)/shard_map/ppermute | solution.py:28
  21.4 0.0 copy-done.5
  21.5 0.9 slice_bitcast_fusion
  22.4 1.4 %collective-permute-start.4 = (bf16[128,1536]{1,0:T(8,128)(2,1)}, bf16[128,1536]{1,0:T(8,128)(2,1)}, u32[]{:S(2)}, u32[]{:S(2)}) collective-permute-start(bf16[128,1536]{1,0:T(8,128)(2,1)} %get-tuple-element.36), channel_id=1, source_target_pairs={{32,96},{160,224},{288,352},{416,480},{33,97},{161,225},{289,353},... | collective-permute-start | bytes 1179656 | tf_op jit(solution)/shard_map/ppermute | solution.py:28
  23.8 25.8 %collective-permute-done.x_ref = bf16[256,1536]{1,0:T(8,128)(2,1)S(1)} collective-permute-done((bf16[256,1536]{1,0:T(8,128)(2,1)}, bf16[256,1536]{1,0:T(8,128)(2,1)S(1)}, u32[]{:S(2)}, u32[]{:S(2)}) %collective-permute-start) | collective-permute-done | bytes 786464 | tf_op jit(solution)/shard_map/ppermute | solution.py:28
  49.7 0.0 copy-start
  49.7 1.2 %local_stats.1 = f32[64,256]{1,0:T(8,128)} custom-call(bf16[256,1536]{1,0:T(8,128)(2,1)S(1)} %collective-permute-done.x_ref), custom_call_target="tpu_custom_call" | custom-call | flops 3145728 | bytes 786432 | tf_op jit(solution)/shard_map/local_stats/pallas_call | solution.py:87
  50.9 6.8 %all-to-all-start = ((f32[8,8,256]{2,1,0:T(8,128)}), f32[8,8,256]{2,1,0:T(8,128)S(1)}, u32[]{:S(2)}, u32[]{:S(2)}) async-start(f32[8,8,256]{2,1,0:T(8,128)} %bitcast.1), calls=%async_computation | async-start | bytes 131072 | tf_op jit(solution)/shard_map/all_to_all | solution.py:100
  57.7 0.0 collective-permute-done.4
  57.7 1.4 %collective-permute-start.5 = (bf16[128,1536]{1,0:T(8,128)(2,1)}, bf16[128,1536]{1,0:T(8,128)(2,1)}, u32[]{:S(2)}, u32[]{:S(2)}) collective-permute-start(bf16[128,1536]{1,0:T(8,128)(2,1)} %collective-permute-done.4), channel_id=1, source_target_pairs={{96,416},{224,288},{352,160},{480,32},{97,417},{225,289},{353,161}... | collective-permute-start | bytes 1179656 | tf_op jit(solution)/shard_map/ppermute | solution.py:28
  59.1 7.5 %collective-permute-done.1.one_ref = bf16[256,1536]{1,0:T(8,128)(2,1)} collective-permute-done((bf16[256,1536]{1,0:T(8,128)(2,1)S(1)}, bf16[256,1536]{1,0:T(8,128)(2,1)}, u32[]{:S(2)}, u32[]{:S(2)}) %collective-permute-start.1) | collective-permute-done | bytes 786464 | tf_op jit(solution)/shard_map/ppermute | solution.py:28
  66.6 0.0 collective-permute-done.2.two_ref
  66.6 1.9 %collective-permute-start.6 = (bf16[256,1536]{1,0:T(8,128)(2,1)S(1)}, bf16[256,1536]{1,0:T(8,128)(2,1)S(1)}, u32[]{:S(2)}, u32[]{:S(2)}) collective-permute-start(bf16[256,1536]{1,0:T(8,128)(2,1)S(1)} %bitcast.32), channel_id=1, source_target_pairs={{0,448},{64,384},{96,352},{128,320},{192,256},{224,224},{256,192},... | collective-permute-start | bytes 2359304 | tf_op jit(solution)/shard_map/ppermute | solution.py:28
  68.5 0.0 all-to-all-done
  68.5 0.0 copy-start.1
  68.6 0.0 copy-done
  68.6 0.6 copy-done.1
  69.2 9.0 %backward_layer.1 = (f32[256,1536]{1,0:T(8,128)}, bf16[256,1536]{1,0:T(8,128)(2,1)}, bf16[256,1536]{1,0:T(8,128)(2,1)}, f32[64,256]{1,0:T(8,128)}, f32[3,1,1536]{2,1,0:T(1,128)}) custom-call(s32[1]{0:T(128)} %bitcast.3.odd_ref, f32[64,256]{1,0:T(8,128)} %bitcast.25, s32[2,256]{1,0:T(2,128)} %bitcast.30, f32[3,1,1536]{2,1,0:T(1,128)} %bitcast.28, ...), custom_call_target="tpu_custom_call" | custom-call | flops 1006632960 | bytes 5505024 | tf_op jit(solution)/shard_map/backward_layer/pallas_call | solution.py:234
  78.2 6.8 %all-to-all-start.1 = ((f32[8,8,256]{2,1,0:T(8,128)}), f32[8,8,256]{2,1,0:T(8,128)S(1)}, u32[]{:S(2)}, u32[]{:S(2)}) async-start(f32[8,8,256]{2,1,0:T(8,128)} %bitcast.33), calls=%async_computation.1 | async-start | bytes 131072 | tf_op jit(solution)/shard_map/all_to_all | solution.py:100
  85.0 0.0 copy-start.2
  85.0 0.0 copy-start.3
  85.0 0.0 copy-start.4
  85.0 7.5 %all-gather = f32[12,1,1536]{2,1,0:T(1,128)S(1)} all-gather(f32[3,1,1536]{2,1,0:T(1,128)} %in_order.1), channel_id=2, replica_groups=mesh['pipe'=16,'tensor'=8,'dp'=4] {'dp'}, dimensions={0}, use_global_device_ids=true | all-gather | bytes 92160 | tf_op jit(solution)/shard_map/all_gather | solution.py:340
  92.5 0.0 all-to-all-done.1
  92.5 0.0 copy-done.2
  92.5 0.0 copy-done.3
  92.5 0.0 copy-done.4
  92.5 0.0 copy-start.6
  92.5 6.0 %finish_layer.1 = (bf16[256,1536]{1,0:T(8,128)(2,1)}, bf16[256,1536]{1,0:T(8,128)(2,1)}, f32[3,1,1536]{2,1,0:T(1,128)}) custom-call(f32[64,256]{1,0:T(8,128)S(1)} %bitcast.26, f32[64,256]{1,0:T(8,128)S(1)} %bitcast.27, s32[2,256]{1,0:T(2,128)S(1)} %bitcast.31, f32[3,1,1536]{2,1,0:T(1,128)S(1)} %bitcast.29, f32[4,3,1,1536]{3,2,1,0:T(1,128)S(1)} %bitcast.24, ...), custom_call_target="tpu_custom_call" | custom-call | flops 402653184 | bytes 5505024 | tf_op jit(solution)/shard_map/finish_layer/pallas_call | solution.py:275
  98.5 0.0 copy-done.6
  98.5 0.7 collective-permute-start.3
  99.2 0.0 collective-permute-done.5
  99.2 0.0 collective-permute-done.3
  99.2 0.0 collective-permute-done.6
  99.2 2.1 %fusion = bf16[1,1,256,1536]{3,2,1,0:T(8,128)(2,1)} fusion(bf16[256,1536]{1,0:T(8,128)(2,1)S(1)} %collective-permute-done.6, bf16[128,1536]{1,0:T(8,128)(2,1)} %collective-permute-done.5, bf16[128,1536]{1,0:T(8,128)(2,1)S(1)} %collective-permute-done.3, pred[]{:T(512)S(6)} %eq.8), kind=kLoop, calls=%fused_computation.1 | loop fusion | flops 1966080 | bytes 2359297 | tf_op jit(solution)/shard_map/broadcast_in_dim | solution.py:348
  (1 shorter events, 0.0 us)
Async XLA Ops:
  0.6 49.0 %collective-permute-start = (bf16[256,1536]{1,0:T(8,128)(2,1)}, bf16[256,1536]{1,0:T(8,128)(2,1)S(1)}, u32[]{:S(2)}, u32[]{:S(2)}) collective-permute-start(bf16[256,1536]{1,0:T(8,128)(2,1)} %bitcast.34), channel_id=1, source_target_pairs={{0,480},{32,448},{64,416},{96,384},{128,352},{160,320},{192,288},{... | collective-permute-start | bytes 2359304 | tf_op jit(solution)/shard_map/ppermute | solution.py:28
  14.6 6.8 %copy-start.5 = (bf16[1,1,256,1536]{3,2,1,0:T(8,128)(2,1)S(1)}, bf16[1,1,256,1536]{3,2,1,0:T(8,128)(2,1)}, u32[]{:S(2)}) copy-start(bf16[1,1,256,1536]{3,2,1,0:T(8,128)(2,1)} %param.5) | copy-start | bytes 2359300
  16.2 50.4 %collective-permute-start.1 = (bf16[256,1536]{1,0:T(8,128)(2,1)S(1)}, bf16[256,1536]{1,0:T(8,128)(2,1)}, u32[]{:S(2)}, u32[]{:S(2)}) collective-permute-start(bf16[256,1536]{1,0:T(8,128)(2,1)S(1)} %get-tuple-element.35), channel_id=1, source_target_pairs={{0,480},{32,64},{64,32},{96,128},{128,96},{160,192},{192,160},{224... | collective-permute-start | bytes 2359304 | tf_op jit(solution)/shard_map/ppermute | solution.py:28
  18.1 48.5 %collective-permute-start.2 = (bf16[256,1536]{1,0:T(8,128)(2,1)S(1)}, bf16[256,1536]{1,0:T(8,128)(2,1)}, u32[]{:S(2)}, u32[]{:S(2)}) collective-permute-start(bf16[256,1536]{1,0:T(8,128)(2,1)S(1)} %get-tuple-element.34), channel_id=1, source_target_pairs={{0,32},{32,0},{64,96},{96,64},{128,160},{160,128},{192,224},{224,1... | collective-permute-start | bytes 2359304 | tf_op jit(solution)/shard_map/ppermute | solution.py:28
  22.4 35.3 %collective-permute-start.4 = (bf16[128,1536]{1,0:T(8,128)(2,1)}, bf16[128,1536]{1,0:T(8,128)(2,1)}, u32[]{:S(2)}, u32[]{:S(2)}) collective-permute-start(bf16[128,1536]{1,0:T(8,128)(2,1)} %get-tuple-element.36), channel_id=1, source_target_pairs={{32,96},{160,224},{288,352},{416,480},{33,97},{161,225},{289,353},... | collective-permute-start | bytes 1179656 | tf_op jit(solution)/shard_map/ppermute | solution.py:28
  49.7 18.9 %copy-start = (bf16[256,1536]{1,0:T(8,128)(2,1)}, bf16[256,1536]{1,0:T(8,128)(2,1)S(1)}, u32[]{:S(2)}) copy-start(bf16[256,1536]{1,0:T(8,128)(2,1)S(1)} %collective-permute-done.x_ref) | copy-start | bytes 2359300
  50.9 17.7 %all-to-all-start = ((f32[8,8,256]{2,1,0:T(8,128)}), f32[8,8,256]{2,1,0:T(8,128)S(1)}, u32[]{:S(2)}, u32[]{:S(2)}) async-start(f32[8,8,256]{2,1,0:T(8,128)} %bitcast.1), calls=%async_computation | async-start | bytes 131072 | tf_op jit(solution)/shard_map/all_to_all | solution.py:100
  57.7 41.5 %collective-permute-start.5 = (bf16[128,1536]{1,0:T(8,128)(2,1)}, bf16[128,1536]{1,0:T(8,128)(2,1)}, u32[]{:S(2)}, u32[]{:S(2)}) collective-permute-start(bf16[128,1536]{1,0:T(8,128)(2,1)} %collective-permute-done.4), channel_id=1, source_target_pairs={{96,416},{224,288},{352,160},{480,32},{97,417},{225,289},{353,161}... | collective-permute-start | bytes 1179656 | tf_op jit(solution)/shard_map/ppermute | solution.py:28
  66.6 32.6 %collective-permute-start.6 = (bf16[256,1536]{1,0:T(8,128)(2,1)S(1)}, bf16[256,1536]{1,0:T(8,128)(2,1)S(1)}, u32[]{:S(2)}, u32[]{:S(2)}) collective-permute-start(bf16[256,1536]{1,0:T(8,128)(2,1)S(1)} %bitcast.32), channel_id=1, source_target_pairs={{0,448},{64,384},{96,352},{128,320},{192,256},{224,224},{256,192},... | collective-permute-start | bytes 2359304 | tf_op jit(solution)/shard_map/ppermute | solution.py:28
  68.5 0.6 copy-start.1
  78.2 14.3 %all-to-all-start.1 = ((f32[8,8,256]{2,1,0:T(8,128)}), f32[8,8,256]{2,1,0:T(8,128)S(1)}, u32[]{:S(2)}, u32[]{:S(2)}) async-start(f32[8,8,256]{2,1,0:T(8,128)} %bitcast.33), calls=%async_computation.1 | async-start | bytes 131072 | tf_op jit(solution)/shard_map/all_to_all | solution.py:100
  85.0 7.5 %copy-start.2 = (f32[8,8,256]{2,1,0:T(8,128)S(1)}, f32[8,8,256]{2,1,0:T(8,128)}, u32[]{:S(2)}) copy-start(f32[8,8,256]{2,1,0:T(8,128)} %copy-done.1) | copy-start | bytes 196612
  85.0 7.5 %copy-start.3 = (f32[1,3,1536]{2,0,1:T(1,128)S(1)}, f32[1,3,1536]{2,0,1:T(1,128)}, u32[]{:S(2)}) copy-start(f32[1,3,1536]{2,0,1:T(1,128)} %param.8) | copy-start | bytes 55300
  85.0 7.5 %copy-start.4 = (s32[1,1,2,256]{3,2,1,0:T(2,128)S(1)}, s32[1,1,2,256]{3,2,1,0:T(2,128)}, u32[]{:S(2)}) copy-start(s32[1,1,2,256]{3,2,1,0:T(2,128)} %param.9) | copy-start | bytes 6148
  92.5 6.0 %copy-start.6 = (bf16[128,1536]{1,0:T(8,128)(2,1)S(1)}, bf16[128,1536]{1,0:T(8,128)(2,1)}, u32[]{:S(2)}) copy-start(bf16[128,1536]{1,0:T(8,128)(2,1)} %get-tuple-element.31) | copy-start | bytes 1179652
  98.5 0.7 collective-permute-start.3
